TPU v7x, 128 devices: a whole 4x4x4 slice. The times are simulated.
128 devices in a mesh: sx: 8 (over x_hi, y), sy: 16 (over x_lo, z, core).
Axes of the slice: x: 4 (x_hi: 2, x_lo: 2; x = x_hi * 2 + x_lo), y: 4, z: 4, core: 2. Of those that a mesh axis runs over, the one named last changes fastest.
Arguments:
- query_rows: bfloat16 [32768, 2048], P(('sx', 'sy')), may hold values from -6 to 6
- key_rows: bfloat16 [32768, 2048], P(('sx', 'sy')), may hold values from -6 to 6
- value_rows: bfloat16 [32768, 2048], P(('sx', 'sy')), may hold values from -48 to 48
- cotangent: bfloat16 [32768, 2048], P(('sx', 'sy')), may hold values from -24 to 24
- out_weight: bfloat16 [2048, 2048], replicated, may hold values from -0.125 to 0.125
- sorted_blocks: int32 [16, 128], replicated, may hold values from 0 to 127, as said below
- window_start: int32 [16, 128], P(None, ('sx', 'sy')), may hold values from 0 to 61
Outputs:
- layer_output: bfloat16 [32768, 2048], P(('sx', 'sy'))
- grad_queries: bfloat16 [32768, 2048], P(('sx', 'sy'))
- grad_keys: bfloat16 [32768, 2048], P(('sx', 'sy'))
- grad_values: bfloat16 [32768, 2048], P(('sx', 'sy'))
- weight_grad: float32 [2048, 2048], P(('sx', 'sy'))
Inputs may be any that keep to these rules, and one draw needn't show every extreme that they name: `sorted_blocks`: block j lies on the device at position j // 1 in sequence order (sx index outer, sy index inner). For each device, the 16 pairs (h, i) of its own query blocks i name blocks on devices of each sx index exactly 2 times. For any device s and any sy index c, at most 2 pairs (h, i) whose block i lies on a device of sy index c name a block on s, and in every draw some s and c reach 2.
All inputs are finite; a program needn't handle non-finite values.
Results may differ from a plain program's by a relative error of at most 0.025.
Values may be sent and summed in bfloat16 or wider, within the bound.
A program may use at most 128 MiB of HBM per device.

v0:
```python
import math

import jax
import jax.numpy as jnp
from jax import lax
from jax.sharding import PartitionSpec as P

HEADS = 16
DH = 128
BLOCK = 256


def group_rank(groups, chosen, group_count):
    onehot = (
        (groups[:, None] == jnp.arange(group_count, dtype=jnp.int32)[None, :]) & chosen[:, None]
    ).astype(jnp.int32)
    before = jnp.cumsum(onehot, axis=0) - onehot
    return jnp.sum(before * onehot, axis=1)


def slot_owner(slot_ids, chosen, labels, slot_width):
    matches = (
        (slot_ids[:, None] == jnp.arange(slot_width, dtype=jnp.int32)[None, :]) & chosen[:, None]
    ).astype(jnp.int32)
    return (jnp.sum(matches * labels[:, None], axis=0), jnp.sum(matches, axis=0))


def per_device(
    query_rows, key_rows, value_rows, cotangent, out_weight, sorted_blocks, window_start
):
    n_outer = lax.axis_size("sx")
    n_inner = lax.axis_size("sy")
    pos_outer = lax.axis_index("sx")
    pos_inner = lax.axis_index("sy")
    device = pos_outer * n_inner + pos_inner
    local_rows = query_rows.shape[0]
    blocks = local_rows // BLOCK
    total_blocks = sorted_blocks.shape[1]
    per_outer = HEADS * blocks // n_outer
    per_inner = 2 * HEADS * blocks // n_inner
    width_first = n_inner * per_inner
    width_second = n_outer * per_outer
    score_scale = 1.0 / math.sqrt(DH)
    pair_width = 2 * DH
    source = (sorted_blocks // blocks).reshape(-1)
    source_local = (sorted_blocks % blocks).reshape(-1)
    head_label = jnp.broadcast_to(
        jnp.arange(HEADS, dtype=jnp.int32)[:, None], sorted_blocks.shape
    ).reshape(-1)
    target = jnp.broadcast_to(
        (jnp.arange(total_blocks, dtype=jnp.int32) // blocks)[None, :], sorted_blocks.shape
    ).reshape(-1)
    source_outer = source // n_inner
    source_inner = source % n_inner
    target_outer = target // n_inner
    target_inner = target % n_inner
    from_here = source == device
    rank_first = group_rank(target_inner, from_here, n_inner)
    send_label, send_used = slot_owner(
        target_inner * per_inner + rank_first,
        from_here,
        head_label * blocks + source_local,
        width_first,
    )
    passing = (source_outer == pos_outer) & (target_inner == pos_inner)
    held_at = source_inner * per_inner + group_rank(source_inner, passing, n_inner)
    slot_second = target_outer * per_outer + group_rank(target_outer, passing, n_outer)
    relay_from, relay_used = slot_owner(slot_second, passing, held_at, width_second)
    mine_blocks = lax.dynamic_slice_in_dim(sorted_blocks, device * blocks, blocks, 1)
    mine_outer = (mine_blocks // blocks // n_inner).reshape(-1)
    everyone = jnp.ones(mine_outer.shape, jnp.bool_)
    landed_at = mine_outer * per_outer + group_rank(mine_outer, everyone, n_outer)
    query_blocks = query_rows.reshape(blocks, BLOCK, HEADS, DH)
    key_blocks = key_rows.reshape(blocks, BLOCK, HEADS, DH)
    value_blocks = value_rows.reshape(blocks, BLOCK, HEADS, DH)
    own_pairs = jnp.concatenate([key_blocks, value_blocks], axis=3).transpose(2, 0, 1, 3)
    pair_table = own_pairs.reshape(HEADS * blocks, BLOCK, pair_width)
    outgoing = jnp.where(
        send_used[:, None, None] > 0, pair_table[send_label], jnp.zeros((), jnp.bfloat16)
    )
    arrived = lax.all_to_all(
        outgoing.reshape(n_inner, per_inner, BLOCK, pair_width),
        "sy",
        split_axis=0,
        concat_axis=0,
        tiled=True,
    )
    relayed = arrived.reshape(width_first, BLOCK, pair_width)[relay_from]
    landed = lax.all_to_all(
        relayed.reshape(n_outer, per_outer, BLOCK, pair_width),
        "sx",
        split_axis=0,
        concat_axis=0,
        tiled=True,
    )
    fetched = landed.reshape(width_second, BLOCK, pair_width)[landed_at].reshape(
        HEADS, blocks, BLOCK, pair_width
    )
    key_set = jnp.concatenate([own_pairs, fetched], axis=2)
    key_part = key_set[..., :DH]
    value_part = key_set[..., DH:]
    key_spots = jnp.arange(BLOCK, dtype=jnp.int32)
    key_seen = jnp.concatenate(
        [
            key_spots[None, None, :] >= window_start[:, :, None],
            jnp.ones((HEADS, blocks, BLOCK), jnp.bool_),
        ],
        axis=2,
    )
    scores = (
        jnp.einsum("jqhd,hjkd->hjqk", query_blocks, key_part, preferred_element_type=jnp.float32)
        * score_scale
    )
    scores = jnp.where(key_seen[:, :, None, :], scores, -jnp.inf)
    row_max = jnp.max(scores, axis=-1, keepdims=True)
    exp_scores = jnp.exp(scores - row_max)
    soft_weights = exp_scores / jnp.sum(exp_scores, axis=-1, keepdims=True)
    weights_b = soft_weights.astype(jnp.bfloat16)
    attended = jnp.einsum(
        "hjqk,hjkd->jqhd", weights_b, value_part, preferred_element_type=jnp.float32
    ).astype(jnp.bfloat16)
    attention = attended.reshape(local_rows, HEADS * DH)
    layer_output = jnp.dot(attention, out_weight, preferred_element_type=jnp.float32).astype(
        jnp.bfloat16
    )
    attention_grad = lax.dot_general(
        cotangent, out_weight, (((1,), (1,)), ((), ())), preferred_element_type=jnp.float32
    ).astype(jnp.bfloat16)
    grad_blocks = attention_grad.reshape(blocks, BLOCK, HEADS, DH)
    row_delta = jnp.sum(grad_blocks.astype(jnp.float32) * attended.astype(jnp.float32), axis=3)
    prob_grad = jnp.einsum(
        "jqhd,hjkd->hjqk", grad_blocks, value_part, preferred_element_type=jnp.float32
    )
    dscore = (soft_weights * (prob_grad - row_delta.transpose(2, 0, 1)[..., None])).astype(
        jnp.bfloat16
    )
    grad_queries = (
        (
            jnp.einsum("hjqk,hjkd->jqhd", dscore, key_part, preferred_element_type=jnp.float32)
            * score_scale
        )
        .astype(jnp.bfloat16)
        .reshape(local_rows, HEADS * DH)
    )
    key_terms = (
        jnp.einsum("hjqk,jqhd->hjkd", dscore, query_blocks, preferred_element_type=jnp.float32)
        * score_scale
    )
    value_terms = jnp.einsum(
        "hjqk,jqhd->hjkd", weights_b, grad_blocks, preferred_element_type=jnp.float32
    )
    all_terms = jnp.concatenate([key_terms, value_terms], axis=3)
    own_terms = all_terms[:, :, :BLOCK]
    sent_terms = (
        all_terms[:, :, BLOCK:].astype(jnp.bfloat16).reshape(HEADS * blocks, BLOCK, pair_width)
    )
    inverse_landed = (
        jnp.zeros((width_second,), jnp.int32)
        .at[landed_at]
        .set(jnp.arange(width_second, dtype=jnp.int32))
    )
    homeward = sent_terms[inverse_landed]
    returned = lax.all_to_all(
        homeward.reshape(n_outer, per_outer, BLOCK, pair_width),
        "sx",
        split_axis=0,
        concat_axis=0,
        tiled=True,
    )
    held_back = (
        jnp.zeros((width_first, BLOCK, pair_width), jnp.bfloat16)
        .at[relay_from]
        .set(returned.reshape(width_second, BLOCK, pair_width))
    )
    reverse_rows = lax.all_to_all(
        held_back.reshape(n_inner, per_inner, BLOCK, pair_width),
        "sy",
        split_axis=0,
        concat_axis=0,
        tiled=True,
    ).reshape(width_first, BLOCK, pair_width)
    assign = (
        (send_label[:, None] == jnp.arange(HEADS * blocks, dtype=jnp.int32)[None, :])
        & (send_used[:, None] > 0)
    ).astype(jnp.bfloat16)
    routed = jnp.einsum(
        "st,sbc->tbc", assign, reverse_rows, preferred_element_type=jnp.float32
    ).reshape(HEADS, blocks, BLOCK, pair_width)
    summed = (own_terms + routed).astype(jnp.bfloat16)
    grad_keys = summed[..., :DH].transpose(1, 2, 0, 3).reshape(local_rows, HEADS * DH)
    grad_values = summed[..., DH:].transpose(1, 2, 0, 3).reshape(local_rows, HEADS * DH)
    tokens_all = local_rows * n_outer * n_inner
    weight_grad = lax.psum_scatter(
        lax.dot_general(
            attention, cotangent, (((0,), (0,)), ((), ())), preferred_element_type=jnp.float32
        ),
        ("sx", "sy"),
        scatter_dimension=0,
        tiled=True,
    )
    weight_grad = weight_grad * (1.0 / math.sqrt(tokens_all))
    return (layer_output, grad_queries, grad_keys, grad_values, weight_grad)


def solution(mesh):
    placed = (
        P(("sx", "sy"), None),
        P(("sx", "sy"), None),
        P(("sx", "sy"), None),
        P(("sx", "sy"), None),
        P(),
        P(),
        P(None, ("sx", "sy")),
    )
    return jax.shard_map(
        per_device,
        mesh=mesh,
        in_specs=placed,
        out_specs=(
            P(("sx", "sy"), None),
            P(("sx", "sy"), None),
            P(("sx", "sy"), None),
            P(("sx", "sy"), None),
            P(("sx", "sy"), None),
        ),
        check_vma=False,
    )
```

profile of v0, /device:TPU:1, one launch (start us, length us, event | category | flops | bytes accessed | tf_op | source)
XLA Modules:
  0.0 847.0 jit_solution(7994539301777492794)
XLA Ops:
  14.2 4.5 reduce-window.20
  19.8 3.4 fusion.18
  23.3 2.7 gather_fusion
  26.0 4.5 broadcast_select_fusion
  30.5 7.9 all-to-all-start
  38.4 4.5 reduce-window.26
  46.9 47.2 %all-to-all-done = bf16[16,2,256,256]{3,2,1,0:T(8,128)(2,1)} async-done(((bf16[16,2,256,256]{3,2,1,0:T(8,128)(2,1)}), bf16[16,2,256,256]{3,2,1,0:T(8,128)(2,1)}, u32[]{:S(2)}, u32[]{:S(2)}) %all-to-all-start) | async-done | bytes 4194336 | tf_op jit(solution)/shard_map/all_to_all | solution.py:81
  94.1 4.2 gather_fusion.1
  98.3 6.4 all-to-all-start.1
  104.9 6.7 convolution_convert_fusion
  117.2 13.8 %all-to-all-done.1 = bf16[8,2,256,256]{3,2,1,0:T(8,128)(2,1)} async-done(((bf16[8,2,256,256]{3,2,1,0:T(8,128)(2,1)}), bf16[8,2,256,256]{3,2,1,0:T(8,128)(2,1)}, u32[]{:S(2)}, u32[]{:S(2)}) %all-to-all-start.1) | async-done | bytes 2097184 | tf_op jit(solution)/shard_map/all_to_all | solution.py:89
  130.9 3.6 gather_fusion.2
  134.5 6.6 fusion.82
  141.1 4.4 fusion.12
  148.4 8.1 fusion.87
  159.7 4.1 convolution_bitcast_fusion
  163.9 5.7 multiply_convert_fusion
  175.1 3.6 gather_fusion.3
  178.7 36.8 %all_to_all.20 = bf16[8,2,256,256]{2,3,1,0:T(8,128)(2,1)} all-to-all(bf16[8,2,256,256]{2,3,1,0:T(8,128)(2,1)} %bitcast.257), channel_id=1, replica_groups=mesh['sx'=8,'sy'=16] {'sx'}, dimensions={0} | all-to-all | bytes 4194304 | tf_op jit(solution)/shard_map/all_to_all | solution.py:163
  215.5 3.9 copy.93
  221.8 6.0 scatter_fusion
  227.8 8.6 %copy.94 = bf16[16,2,256,256]{3,1,2,0:T(2,128)(2,1)} copy(bf16[16,2,256,256]{3,2,1,0:T(8,128)(2,1)} %bitcast.248) | data formatting | bytes 8388608 | tf_op jit(solution)/shard_map/reshape | solution.py:176
  236.4 12.5 %all-to-all-start.3 = ((bf16[16,2,256,256]{3,1,2,0:T(2,128)(2,1)}), bf16[16,2,256,256]{3,1,2,0:T(2,128)(2,1)}, u32[]{:S(2)}, u32[]{:S(2)}) async-start(bf16[16,2,256,256]{3,1,2,0:T(2,128)(2,1)} %copy.94), calls=%async_computation.3 | async-start | bytes 8388608 | tf_op jit(solution)/shard_map/all_to_all | solution.py:175
  248.8 4.5 multiply_convert_fusion.1
  255.6 6.7 convolution_convert_fusion.1
  262.3 44.7 %all-to-all-done.3 = bf16[16,2,256,256]{3,1,2,0:T(2,128)(2,1)} async-done(((bf16[16,2,256,256]{3,1,2,0:T(2,128)(2,1)}), bf16[16,2,256,256]{3,1,2,0:T(2,128)(2,1)}, u32[]{:S(2)}, u32[]{:S(2)}) %all-to-all-start.3) | async-done | bytes 4194336 | tf_op jit(solution)/shard_map/all_to_all | solution.py:175
  307.0 9.0 %copy.95 = bf16[16,2,256,256]{3,1,0,2:T(2,128)(2,1)} copy(bf16[16,2,256,256]{3,1,2,0:T(2,128)(2,1)} %all-to-all-done.3) | data formatting | bytes 8388608 | tf_op jit(solution)/shard_map/all_to_all | solution.py:175
  315.9 7.2 reshape.484
  323.2 5.0 fusion.59
  328.1 5.3 copy.96
  333.4 4.2 fusion.7
  340.6 498.0 %reduce-scatter.2.cloned.1.call-done = f32[16,2048]{1,0:T(8,128)} async-done(((f32[2048,2048]{1,0:T(8,128)}), f32[16,2048]{1,0:T(8,128)}) %reduce-scatter.2.cloned.1.call-update) | async-done | bytes 131088 | tf_op jit(solution)/shard_map/reduce_scatter | solution.py:193
  (103 shorter events, 38.4 us)
Async XLA Ops:
  7.2 97.7 %copy-start = (bf16[256,2048]{1,0:T(8,128)(2,1)S(1)}, bf16[256,2048]{1,0:T(8,128)(2,1)}, u32[]{:S(2)}) copy-start(bf16[256,2048]{1,0:T(8,128)(2,1)} %param.10) | copy-start | bytes 3145732
  7.2 5.1 copy-start.15
  30.5 16.0 %copy-start.16 = (s32[16,128]{1,0:T(8,128)S(1)}, s32[16,128]{1,0:T(8,128)}, u32[]{:S(2)}) copy-start(s32[16,128]{1,0:T(8,128)} %param.12) | copy-start | bytes 24580
  30.5 63.6 %all-to-all-start = ((bf16[16,2,256,256]{3,2,1,0:T(8,128)(2,1)}), bf16[16,2,256,256]{3,2,1,0:T(8,128)(2,1)}, u32[]{:S(2)}, u32[]{:S(2)}) async-start(bf16[16,2,256,256]{3,2,1,0:T(8,128)(2,1)} %broadcast_select_fusion), calls=%async_computation | async-start | bytes 8388608 | tf_op jit(solution)/shard_map/all_to_all | solution.py:81
  98.3 32.6 %all-to-all-start.1 = ((bf16[8,2,256,256]{3,2,1,0:T(8,128)(2,1)}), bf16[8,2,256,256]{3,2,1,0:T(8,128)(2,1)}, u32[]{:S(2)}, u32[]{:S(2)}) async-start(bf16[8,2,256,256]{3,2,1,0:T(8,128)(2,1)} %bitcast.16), calls=%async_computation.1 | async-start | bytes 4194304 | tf_op jit(solution)/shard_map/all_to_all | solution.py:89
  104.7 733.9 %reduce-scatter.2.cloned.1.call-start = ((), (), s32[]{:S(2)}) async-start(), calls=%async_computation.5 | async-start | bytes 16908288 | tf_op jit(solution)/shard_map/reduce_scatter | solution.py:193
  111.6 5.5 copy-start.17
  111.6 22.9 %copy-start.5 = (bf16[16,1,256,256]{3,2,0,1:T(8,128)(2,1)S(1)}, bf16[16,1,256,256]{3,2,0,1:T(8,128)(2,1)}, u32[]{:S(2)}) copy-start(bf16[16,1,256,256]{3,2,0,1:T(8,128)(2,1)} %get-tuple-element.29) | copy-start | bytes 6291460
  141.1 4.4 copy-start.6
  141.1 4.6 copy-start.11
  145.5 2.0 copy-start.4
  147.5 1.0 copy-start.9
  156.5 1.2 copy-start.13
  159.7 4.2 copy-start.7
  159.7 4.2 copy-start.14
  163.8 7.3 copy-start.2
  163.9 5.7 copy-start.12
  169.6 2.0 copy-start.8
  171.6 1.9 copy-start.3
  236.4 70.6 %all-to-all-start.3 = ((bf16[16,2,256,256]{3,1,2,0:T(2,128)(2,1)}), bf16[16,2,256,256]{3,1,2,0:T(2,128)(2,1)}, u32[]{:S(2)}, u32[]{:S(2)}) async-start(bf16[16,2,256,256]{3,1,2,0:T(2,128)(2,1)} %copy.94), calls=%async_computation.3 | async-start | bytes 8388608 | tf_op jit(solution)/shard_map/all_to_all | solution.py:175
  248.8 6.7 copy-start.10
  333.4 506.8 %copy-start.1 = (bf16[256,2048]{1,0:T(8,128)(2,1)S(1)}, bf16[256,2048]{1,0:T(8,128)(2,1)}, u32[]{:S(2)}) copy-start(bf16[256,2048]{1,0:T(8,128)(2,1)} %param.10) | copy-start | bytes 3145732
Sparse Core Ops, SparseCore 0:
  156.7 681.8 reduce-scatter.1
where the time goes:
time: 851 us; the launch traced here: 847 us
  waiting for transfers between devices  604 us (71%)
  local copies, waits for them, and re-layouts  80.2 us (9%)
  matrix products  49.8 us (6%)
  blocking collectives  36.8 us (4%)
  other arithmetic  35.2 us (4%)
  starting transfers between devices  26.9 us (3%)
  between operations  14.4 us (2%)
    reduce_scatter x1, waiting for transfers between devices, per_device(): lax.psum_scatter(lax.dot_general(attention, cotangent, (((0,), (0,)), (()...  498 us
    all_to_all x1, waiting for transfers between devices, per_device(): lax.all_to_all(outgoing.reshape(n_inner, per_inner, BLOCK, pair_width), '...  47.2 us
    all_to_all x1, waiting for transfers between devices, per_device(): lax.all_to_all(held_back.reshape(n_inner, per_inner, BLOCK, pair_width),...  44.7 us
    all_to_all x1, blocking collectives, per_device(): lax.all_to_all(homeward.reshape(n_outer, per_outer, BLOCK, pair_width), '...  36.8 us
  transfers between devices with their start and end apart: 4, of which 4 were waited for; matrix products, arithmetic and copies ran while one was open for 13% of the time, Pallas kernels for 0%

commit v1 on v0

v1 whole, which is shorter than its diff:
```python
import math

import jax
import jax.numpy as jnp
from jax import lax
from jax.experimental import pallas as pl
from jax.experimental.pallas import tpu as pltpu
from jax.sharding import PartitionSpec as P

HEADS = 16
DH = 128
BLOCK = 256
DIM = 2048
PARTS = 8
HALF = PARTS // 2
ROWS = BLOCK // HALF
AHEAD = 2
SCALE = 1.0 / math.sqrt(DH)
MESH = pl.DeviceIdType.MESH
STREAMS = ((0, 1024, "yzx"), (1024, 512, "xyz"), (1536, 512, "zxy"))
VMEM = pl.BlockSpec(memory_space=pltpu.VMEM)
SMEM = pl.BlockSpec(memory_space=pltpu.SMEM)
ANY = pl.BlockSpec(memory_space=pl.ANY)
NT = (((1,), (1,)), ((), ()))
TN = (((0,), (0,)), ((), ()))
F32 = jnp.float32
BF16 = jnp.bfloat16
T_OUT, T_X, T_BACK, T_Y, T_SLOT, T_HEAD, T_USED = 0, 32, 64, 96, 128, 160, 192


def here():
    outer = lax.axis_index("sx")
    inner = lax.axis_index("sy")
    return (outer // 4) * 2 + inner // 8, outer % 4, (inner // 2) % 4, inner % 2


def place(x, y, z, k):
    return {"sx": (x // 2) * 4 + y, "sy": (x % 2) * 8 + z * 2 + k}


def step_x(pos, d):
    return place((pos[0] + d) % 4, pos[1], pos[2], pos[3])


def step_y(pos, d):
    return place(pos[0], (pos[1] + d) % 4, pos[2], pos[3])


def step_z(pos, dz, dk):
    return place(pos[0], pos[1], (pos[2] + dz) % 4, (pos[3] + dk) % 2)


def greet(pos):
    barrier = pltpu.get_barrier_semaphore()
    peers = [step_x(pos, d) for d in (1, 2, 3)] + [step_y(pos, d) for d in (1, 2, 3)]
    peers += [step_z(pos, j // 2, j % 2) for j in range(1, 8)]
    for peer in peers:
        pl.semaphore_signal(barrier, inc=1, device_id=peer, device_id_type=MESH)
    pl.semaphore_wait(barrier, len(peers))


def send(src, dst, send_sem, recv_sem, peer):
    pltpu.make_async_remote_copy(
        src_ref=src,
        dst_ref=dst,
        send_sem=send_sem,
        recv_sem=recv_sem,
        device_id=peer,
        device_id_type=MESH,
    ).start()


def settle(ref, sem):
    pltpu.make_async_copy(ref, ref, sem).wait()


def table_kernel(src_ref, out_ref):
    x, y, z, k = here()
    device = lax.axis_index("sx") * 16 + lax.axis_index("sy")
    src = src_ref[...]
    head = lax.broadcasted_iota(jnp.int32, src.shape, 0)
    target = lax.broadcasted_iota(jnp.int32, src.shape, 1)
    outer = src >> 4
    nth = jnp.zeros_like(src)
    for h in range(HEADS):
        nth += jnp.where((outer[h : h + 1] == outer) & (head > h), 1, 0)
    rank = jnp.zeros_like(src)
    for d in range(8):
        turned = pltpu.roll(src, 16 * d, axis=1) if d else src
        for h in range(HEADS):
            first = head > h
            if d:
                first = first | ((head == h) & (target >= 16 * d))
            rank += jnp.where((turned[h : h + 1] == src) & first, 1, 0)
    tx = (target >> 6) * 2 + ((target >> 3) & 1)
    ty, tz, tk = (target >> 4) & 3, (target >> 1) & 3, target & 1
    sx = (src >> 6) * 2 + ((src >> 3) & 1)
    sy, sz, sk = (src >> 4) & 3, (src >> 1) & 3, src & 1
    column = (tz == z) & (tk == k)
    to_slot = (tx & 1) * 2 + rank
    out_slot = (((tz - z) & 3) * 2 + (tk ^ k)) * 4 + to_slot
    in_slot = (((z - sz) & 3) * 2 + (k ^ sk)) * 4 + to_slot
    x_slot = ((tx - x) & 3) * 8 + ((ty - y) & 3) * 2 + nth
    passing = column & ((src >> 3) == (device >> 3))
    y_slot = ((ty - y) & 3) * 4 + (sx >> 1) * 2 + nth
    y_from = ((x - sx) & 3) * 8 + ((ty - y) & 3) * 2 + nth
    handing = column & (tx == x) & (sy == y)
    mine = target == device
    my_slot = ((y - sy) & 3) * 4 + (sx >> 1) * 2 + nth
    entries = lax.broadcasted_iota(jnp.int32, (32, 128), 0)
    sums = []
    for chosen, spot, value in (
        (src == device, out_slot, head),
        (passing, x_slot, in_slot),
        (passing, in_slot, x_slot),
        (handing, y_slot, y_from),
        (mine, head, my_slot),
        (mine, my_slot, head),
        (src == device, out_slot, head + 1),
    ):
        spot = jnp.where(chosen, spot, -1)
        total = jnp.zeros((32, 128), jnp.int32)
        for h in range(HEADS):
            total += jnp.where(spot[h : h + 1] == entries, value[h : h + 1], 0)
        sums.append(total.astype(F32))
    sums.append(jnp.zeros((32, 128), F32))
    rows = lax.dot_general(
        jnp.ones((8, 128), F32), jnp.concatenate(sums, axis=0), NT, preferred_element_type=F32
    )
    out_ref[...] = rows.astype(jnp.int32)


def make_tables(sorted_blocks):
    return pl.pallas_call(
        table_kernel,
        out_shape=jax.ShapeDtypeStruct((8, 256), jnp.int32),
        in_specs=[VMEM],
        out_specs=VMEM,
    )(sorted_blocks)


def fetch_kernel(
    tab, key, value, cot, weight, landed, grad, cot_other, *scratch
):
    zr, xr, scratch = scratch[:PARTS], scratch[PARTS : 2 * PARTS], scratch[2 * PARTS :]
    wbuf, kv, zs, xs, ys, zss, zrs, xss, xrs, yss, yrs, ysl, cs, cr, wsem = scratch
    pos = here()
    load_w = pltpu.make_async_copy(weight, wbuf, wsem)
    load_w.start()

    def gather_z(p):
        ref = key if p < HALF else value
        rows = pl.ds((p % HALF) * ROWS, ROWS)

        for h in range(HEADS):
            kv[p, h] = ref[rows, h * DH : (h + 1) * DH]

        def piece(n):
            return kv[p, tab[0, T_OUT + n]]

        def own(n, _):
            zr[p][n] = piece(n)
            return _

        def other(n, _):
            zs[p, n - 4] = piece(n)
            return _

        lax.fori_loop(0, 4, own, 0)
        lax.fori_loop(4, 32, other, 0)

    def send_z(p):
        for j in range(1, 8):
            send(
                zs.at[p, pl.ds((j - 1) * 4, 4)], zr[p].at[pl.ds(j * 4, 4)],
                zss.at[p], zrs.at[p], step_z(pos, j // 2, j % 2),
            )

    def pass_x(p):
        settle(zr[p].at[pl.ds(4, 28)], zrs.at[p])

        def own(n, _):
            xr[p][n] = zr[p][tab[0, T_X + n]]
            return _

        def other(n, _):
            xs[p, n - 8] = zr[p][tab[0, T_X + n]]
            return _

        lax.fori_loop(8, 32, other, 0)
        for d in range(1, 4):
            send(
                xs.at[p, pl.ds((d - 1) * 8, 8)], xr[p].at[pl.ds(d * 8, 8)],
                xss.at[p], xrs.at[p], step_x(pos, d),
            )
        lax.fori_loop(0, 8, own, 0)

    def pass_y(p):
        settle(xr[p].at[pl.ds(8, 24)], xrs.at[p])

        def each(n, _):
            ys[p, n] = xr[p][tab[0, T_Y + n]]
            return _

        lax.fori_loop(0, 16, each, 0)
        for d in range(1, 4):
            send(
                ys.at[p, pl.ds(d * 4, 4)], landed.at[p, pl.ds(d * 4, 4)],
                yss.at[p], yrs.at[p], step_y(pos, d),
            )
        pltpu.make_async_copy(
            ys.at[p, pl.ds(0, 4)], landed.at[p, pl.ds(0, 4)], ysl.at[p]
        ).start()

    gather_z(0)
    greet(pos)
    send_z(0)
    for p in range(1, AHEAD):
        gather_z(p)
        send_z(p)
    send(cot, cot_other, cs, cr, step_z(pos, 0, 1))
    for p in range(AHEAD, PARTS):
        gather_z(p)
    load_w.wait()

    def grad_tile(c, _):
        cols = pl.ds(pl.multiple_of(c * 256, 256), 256)
        grad[:, cols] = lax.dot_general(
            cot[...], wbuf[cols, :], NT, preferred_element_type=F32
        ).astype(BF16)
        return _

    lax.fori_loop(0, 8, grad_tile, 0)
    for p in range(PARTS):
        pass_x(p)
        if p + AHEAD < PARTS:
            send_z(p + AHEAD)
        if p >= 1:
            pass_y(p - 1)
    pass_y(PARTS - 1)
    for p in range(PARTS):
        settle(landed.at[p, pl.ds(4, 12)], yrs.at[p])
        settle(landed.at[p, pl.ds(0, 4)], ysl.at[p])
        settle(zs.at[p], zss.at[p])
        settle(xs.at[p], xss.at[p])
        settle(ys.at[p, pl.ds(4, 12)], yss.at[p])
    settle(cot_other, cr)
    settle(cot, cs)


def fetch(tab, key, value, cot, weight):
    slot = (ROWS, DH)
    sems = [pltpu.SemaphoreType.DMA((PARTS,))] * 7 + [pltpu.SemaphoreType.DMA] * 3
    return pl.pallas_call(
        fetch_kernel,
        out_shape=(
            jax.ShapeDtypeStruct((PARTS, 16, *slot), BF16),
            jax.ShapeDtypeStruct((BLOCK, DIM), BF16),
            jax.ShapeDtypeStruct((BLOCK, DIM), BF16),
        ),
        in_specs=[SMEM, VMEM, VMEM, VMEM, ANY],
        out_specs=(VMEM, VMEM, VMEM),
        scratch_shapes=[
            *[pltpu.VMEM((32, *slot), BF16)] * (2 * PARTS),
            pltpu.VMEM((DIM, DIM), BF16),
            pltpu.VMEM((PARTS, HEADS, *slot), BF16),
            pltpu.VMEM((PARTS, 28, *slot), BF16),
            pltpu.VMEM((PARTS, 24, *slot), BF16),
            pltpu.VMEM((PARTS, 16, *slot), BF16),
            *sems,
        ],
        compiler_params=pltpu.CompilerParams(
            collective_id=0, has_side_effects=True, vmem_limit_bytes=58 << 20
        ),
        name="fetch",
    )(tab, key, value, cot, weight)


def attend_kernel(
    tab, start, query, key, value, grad, landed,
    att, att_t, grad_q, own_k, own_v, terms,
):
    h = pl.program_id(0)
    q, g = query[...], grad[...]
    keys = jnp.concatenate([key[...], landed[:HALF, 0].reshape(BLOCK, DH)], axis=0)
    values = jnp.concatenate([value[...], landed[HALF:, 0].reshape(BLOCK, DH)], axis=0)
    scores = lax.dot_general(q, keys, NT, preferred_element_type=F32) * SCALE
    spot = lax.broadcasted_iota(jnp.int32, scores.shape, 1)
    seen = (spot >= BLOCK) | (spot >= start[h, 0])
    scores = jnp.where(seen, scores, -jnp.inf)
    e = jnp.exp(scores - jnp.max(scores, axis=1, keepdims=True))
    probs = e * (1.0 / jnp.sum(e, axis=1, keepdims=True))
    probs_b = probs.astype(BF16)
    a32 = jnp.dot(probs_b, values, preferred_element_type=F32)
    a = a32.astype(BF16)
    att[...] = a
    att_t[...] = a.astype(F32).T.astype(BF16).reshape(1, 4, 2, 16, BLOCK)
    delta = jnp.sum(g.astype(F32) * a.astype(F32), axis=1, keepdims=True)
    pg = lax.dot_general(g, values, NT, preferred_element_type=F32)
    ds = (probs * (pg - delta)).astype(BF16)
    grad_q[...] = (jnp.dot(ds, keys, preferred_element_type=F32) * SCALE).astype(BF16)
    kt = lax.dot_general(ds, q, TN, preferred_element_type=F32) * SCALE
    vt = lax.dot_general(probs_b, g, TN, preferred_element_type=F32)
    own_k[...] = kt[:BLOCK]
    own_v[...] = vt[:BLOCK]
    terms[:HALF, 0] = kt[BLOCK:].astype(BF16).reshape(HALF, ROWS, DH)
    terms[HALF:, 0] = vt[BLOCK:].astype(BF16).reshape(HALF, ROWS, DH)


def attend(tab, start, query, key, value, grad, landed):
    head = pl.BlockSpec((BLOCK, DH), lambda h, tab, start: (0, h))
    slot = pl.BlockSpec(
        (PARTS, 1, ROWS, DH), lambda h, tab, start: (0, tab[0, T_SLOT + h], 0, 0)
    )
    turned = pl.BlockSpec((1, 4, 2, 16, BLOCK), lambda h, tab, start: (h, 0, 0, 0, 0))
    return pl.pallas_call(
        attend_kernel,
        out_shape=(
            jax.ShapeDtypeStruct((BLOCK, DIM), BF16),
            jax.ShapeDtypeStruct((HEADS, 4, 2, 16, BLOCK), BF16),
            jax.ShapeDtypeStruct((BLOCK, DIM), BF16),
            jax.ShapeDtypeStruct((BLOCK, DIM), F32),
            jax.ShapeDtypeStruct((BLOCK, DIM), F32),
            jax.ShapeDtypeStruct((PARTS, 16, ROWS, DH), BF16),
        ),
        grid_spec=pltpu.PrefetchScalarGridSpec(
            num_scalar_prefetch=2,
            grid=(HEADS,),
            in_specs=[head, head, head, head, slot],
            out_specs=[head, turned, head, head, head, slot],
        ),
        compiler_params=pltpu.CompilerParams(vmem_limit_bytes=40 << 20),
        name="attend",
    )(tab, start, query, key, value, grad, landed)


AXES = "xyz"


def pick(order, axis, index):
    spot = [slice(None)] * 5
    spot[order.index(axis)] = index
    return tuple(spot[: len(order)])


def return_kernel(
    tab, terms, att, att_t, cot, cot_other, weight,
    back, layer, wgrad, *scratch,
):
    xb, scratch = scratch[:PARTS], scratch[PARTS:]
    (
    wbuf, at_other, yb, zs, g0, g1, g2, r10, r11, r12, s10, s11, s12,
    r20, r21, r22, s20, s21, s22, r30, r31, r32,
    yss, yrs, ysl, xss, xrs, zss, zrs, zsl, as_, ar, ws, rs, rr,
    ) = scratch
    pos = here()
    coord = dict(zip(AXES, pos[:3]))
    k = pos[3]
    go = {"x": step_x, "y": step_y, "z": lambda pos, d: step_z(pos, d, 0)}
    g, r1, s1 = (g0, g1, g2), (r10, r11, r12), (s10, s11, s12)
    r2, s2, r3 = (r20, r21, r22), (s20, s21, s22), (r30, r31, r32)
    load_w = pltpu.make_async_copy(weight, wbuf, ws)
    load_w.start()
    greet(pos)
    send(att_t.at[:, :, 1 - k], at_other, as_, ar, step_z(pos, 0, 1))
    for p in range(PARTS):
        for d in range(1, 4):
            send(
                terms.at[p, pl.ds(d * 4, 4)], yb.at[p, d], yss.at[p], yrs.at[p],
                step_y(pos, 4 - d),
            )
        pltpu.make_async_copy(terms.at[p, pl.ds(0, 4)], yb.at[p, 0], ysl.at[p]).start()
    settle(at_other, ar)

    for n, (first, width, order) in enumerate(STREAMS):

        def tile(m, c, n=n, first=first):
            cols = pl.ds(pl.multiple_of(first + c * 256, 256), 256)
            mine = att_t[pl.ds(m * 4, 4), :, k].reshape(256, BLOCK)
            theirs = at_other[pl.ds(m * 4, 4)].reshape(256, BLOCK)
            t = jnp.dot(mine, cot[:, cols], preferred_element_type=F32)
            t += jnp.dot(theirs, cot_other[:, cols], preferred_element_type=F32)
            t = t.astype(BF16).reshape(4, 4, 16, 256)
            out = pl.ds(pl.multiple_of(c * 256, 256), 256)
            for i in range(4):
                g[n][(m // 2) * 2 + i % 2, (m % 2) * 2 + i // 2, :, :, out] = t[i]

        def tiles(i, _, tile=tile, n=n, first=first):
            tile(i % 4, i // 4)
            return _

        lax.fori_loop(0, 4 * (width // 256), tiles, 0)
        a = order[0]
        for d in range(1, 4):
            send(
                g[n].at[pick(AXES, a, (coord[a] + d) % 4)], r1[n].at[d - 1],
                rs.at[n, 0], rr.at[n, 0], go[a](pos, d),
            )

    def return_x(p):
        settle(yb.at[p, pl.ds(1, 3)], yrs.at[p])
        settle(yb.at[p, 0], ysl.at[p])
        for d in range(4):
            half = ((pos[0] + 4 - d) % 4) // 2
            src = yb.at[p, :, pl.ds(half * 2, 2)]
            if d:
                send(src, xb[p].at[d], xss.at[p], xrs.at[p], step_x(pos, 4 - d))
            else:
                xb[p][0] = yb[p, :, pl.ds(half * 2, 2)]

    def return_z(p):
        settle(xb[p].at[pl.ds(1, 3)], xrs.at[p])

        def each(n, _):
            e = tab[0, T_BACK + n]
            zs[p, n] = xb[p][e // 8, (e // 2) % 4, e % 2]
            return _

        lax.fori_loop(0, 32, each, 0)
        for j in range(1, 8):
            send(
                zs.at[p, pl.ds(j * 4, 4)], back.at[p, pl.ds(j * 4, 4)],
                zss.at[p], zrs.at[p], step_z(pos, 4 - j // 2, j % 2),
            )
        pltpu.make_async_copy(
            zs.at[p, pl.ds(0, 4)], back.at[p, pl.ds(0, 4)], zsl.at[p]
        ).start()

    def sum_one(n):
        order = STREAMS[n][2]
        a = order[0]
        rest = [b for b in AXES if b != a]
        settle(r1[n], rr.at[n, 0])
        settle(r1[n], rs.at[n, 0])

        def each(i, _):
            at = (i // 4, i % 4)
            spot = list(at)
            spot.insert(AXES.index(a), coord[a])
            t = g[n][tuple(spot)].astype(F32)
            for d in range(3):
                t += r1[n][(d, *at)].astype(F32)
            s1[n][at] = t.astype(BF16)
            return _

        lax.fori_loop(0, 16, each, 0)
        b = order[1]
        for d in range(1, 4):
            send(
                s1[n].at[pick(rest, b, (coord[b] + d) % 4)], r2[n].at[d - 1],
                rs.at[n, 1], rr.at[n, 1], go[b](pos, d),
            )

    def sum_two(n):
        order = STREAMS[n][2]
        rest = [b for b in AXES if b != order[0]]
        settle(r2[n], rr.at[n, 1])
        settle(r2[n], rs.at[n, 1])
        b, c = order[1], order[2]
        for i in range(4):
            spot = [i]
            spot.insert(rest.index(b), coord[b])
            t = s1[n][tuple(spot)].astype(F32)
            for d in range(3):
                t += r2[n][d, i].astype(F32)
            s2[n][i] = t.astype(BF16)
        for d in range(1, 4):
            send(
                s2[n].at[(coord[c] + d) % 4], r3[n].at[d - 1],
                rs.at[n, 2], rr.at[n, 2], go[c](pos, d),
            )

    def sum_three(n):
        first, width, order = STREAMS[n]
        settle(r3[n], rr.at[n, 2])
        settle(r3[n], rs.at[n, 2])
        t = s2[n][coord[order[2]]].astype(F32)
        for d in range(3):
            t += r3[n][d].astype(F32)
        wgrad[:, pl.ds(first, width)] = t * (1.0 / math.sqrt(BLOCK * 128))

    load_w.wait()

    def layer_tile(c, _):
        cols = pl.ds(pl.multiple_of(c * 256, 256), 256)
        layer[:, cols] = jnp.dot(
            att[...], wbuf[:, cols], preferred_element_type=F32
        ).astype(BF16)
        return _

    for p in range(PARTS):
        return_x(p)
        if p == 0:
            lax.fori_loop(0, 8, layer_tile, 0)
        if p >= 1:
            return_z(p - 1)
        if p == 4:
            for n in range(3):
                sum_one(n)
        if p == 6:
            for n in range(3):
                sum_two(n)
    return_z(PARTS - 1)
    for n in range(3):
        sum_three(n)
    for p in range(PARTS):
        settle(back.at[p, pl.ds(4, 28)], zrs.at[p])
        settle(back.at[p, pl.ds(0, 4)], zsl.at[p])
        settle(zs.at[p, pl.ds(4, 28)], zss.at[p])
        settle(xb[p].at[pl.ds(1, 3)], xss.at[p])
        settle(yb.at[p, pl.ds(1, 3)], yss.at[p])
    settle(at_other, as_)


def give_back(tab, terms, att, att_t, cot, cot_other, weight):
    slot = (ROWS, DH)
    widths = [w for _, w, _ in STREAMS]
    per_stream = [
        [pltpu.VMEM((*lead, 16, w), BF16) for w in widths]
        for lead in ((4, 4, 4), (3, 4, 4), (4, 4), (3, 4), (4,), (3,))
    ]
    return pl.pallas_call(
        return_kernel,
        out_shape=(
            jax.ShapeDtypeStruct((PARTS, 32, *slot), BF16),
            jax.ShapeDtypeStruct((BLOCK, DIM), BF16),
            jax.ShapeDtypeStruct((16, DIM), F32),
        ),
        in_specs=[SMEM, VMEM, VMEM, VMEM, VMEM, VMEM, ANY],
        out_specs=(VMEM, VMEM, VMEM),
        scratch_shapes=[
            *[pltpu.VMEM((4, 4, 2, *slot), BF16)] * PARTS,
            pltpu.VMEM((DIM, DIM), BF16),
            pltpu.VMEM((HEADS, 4, 16, BLOCK), BF16),
            pltpu.VMEM((PARTS, 4, 4, *slot), BF16),
            pltpu.VMEM((PARTS, 32, *slot), BF16),
            *[buf for level in per_stream for buf in level],
            *[pltpu.SemaphoreType.DMA((PARTS,))] * 8,
            *[pltpu.SemaphoreType.DMA] * 3,
            pltpu.SemaphoreType.DMA((3, 3)),
            pltpu.SemaphoreType.DMA((3, 3)),
        ],
        compiler_params=pltpu.CompilerParams(
            collective_id=1, has_side_effects=True, vmem_limit_bytes=58 << 20
        ),
        name="give_back",
    )(tab, terms, att, att_t, cot, cot_other, weight)


def final_kernel(tab, back_k, back_v, own_k, own_v, grad_k, grad_v, sum_k, sum_v):
    sum_k[...] = own_k[...]
    sum_v[...] = own_v[...]

    def add(n, _):
        h = tab[0, T_USED + n]

        @pl.when(h > 0)
        def _add():
            cols = pl.ds(pl.multiple_of((h - 1) * DH, DH), DH)
            sum_k[:, cols] += back_k[0, n].astype(F32)
            sum_v[:, cols] += back_v[0, n].astype(F32)

        return _

    lax.fori_loop(0, 32, add, 0)
    grad_k[...] = sum_k[...].astype(BF16)
    grad_v[...] = sum_v[...].astype(BF16)


def finish(tab, back, own_k, own_v):
    rows = pl.BlockSpec((ROWS, DIM), lambda p, tab: (p, 0))
    return pl.pallas_call(
        final_kernel,
        out_shape=(
            jax.ShapeDtypeStruct((BLOCK, DIM), BF16),
            jax.ShapeDtypeStruct((BLOCK, DIM), BF16),
        ),
        grid_spec=pltpu.PrefetchScalarGridSpec(
            num_scalar_prefetch=1,
            grid=(HALF,),
            in_specs=[
                pl.BlockSpec((1, 32, ROWS, DH), lambda p, tab: (p, 0, 0, 0)),
                pl.BlockSpec((1, 32, ROWS, DH), lambda p, tab: (p + HALF, 0, 0, 0)),
                rows,
                rows,
            ],
            out_specs=[rows, rows],
            scratch_shapes=[pltpu.VMEM((ROWS, DIM), F32)] * 2,
        ),
        compiler_params=pltpu.CompilerParams(vmem_limit_bytes=40 << 20),
        name="finish",
    )(tab, back, back, own_k, own_v)


def per_device(
    query_rows, key_rows, value_rows, cotangent, out_weight, sorted_blocks, window_start
):
    tab = make_tables(sorted_blocks)
    landed, grad, cot_other = fetch(tab, key_rows, value_rows, cotangent, out_weight)
    att, att_t, grad_q, own_k, own_v, terms = attend(
        tab, window_start, query_rows, key_rows, value_rows, grad, landed
    )
    back, layer, wgrad = give_back(tab, terms, att, att_t, cotangent, cot_other, out_weight)
    grad_k, grad_v = finish(tab, back, own_k, own_v)
    return layer, grad_q, grad_k, grad_v, wgrad


def solution(mesh):
    rows = P(("sx", "sy"), None)
    return jax.shard_map(
        per_device,
        mesh=mesh,
        in_specs=(rows, rows, rows, rows, P(), P(), P(None, ("sx", "sy"))),
        out_specs=(rows, rows, rows, rows, rows),
        check_vma=False,
    )
```

time: 851 us -> 203 us (0.24)
  waiting for transfers between devices: 604 us -> 0 us
  Pallas kernels: 0 us -> 191 us
  local copies, waits for them, and re-layouts: 80.2 us -> 10.4 us
  matrix products: 49.8 us -> 0 us
  blocking collectives: 36.8 us -> 0 us
  other arithmetic: 35.2 us -> 0 us
  starting transfers between devices: 26.9 us -> 0 us
  between operations: 14.4 us -> 0.73 us
    reduce_scatter x1 -> x0, waiting for transfers between devices: 498 us -> none  [per_device(): lax.psum_scatter(lax.dot_general(attention, cotangent, (((0,), (0,)), (()...]
    pallas_call x0 -> x5, Pallas kernels: none -> 191 us  [the longest x1 89.1 us: give_back(): pl.pallas_call(return_kernel, out_shape=(jax.ShapeDtypeStruct((PARTS, 32,...]
    all_to_all x3 -> x0, waiting for transfers between devices: 106 us -> none  [the longest x1 47.2 us: per_device(): lax.all_to_all(outgoing.reshape(n_inner, per_inner, BLOCK, pair_width), '...]
    dot_general x9 -> x0, matrix products: 43.1 us -> none  [the longest x1 8.07 us: per_device(): lax.dot_general(attention, cotangent, (((0,), (0,)), ((), ())), preferred...]
    all_to_all x1 -> x0, blocking collectives: 36.8 us -> none  [per_device(): lax.all_to_all(homeward.reshape(n_outer, per_outer, BLOCK, pair_width), '...]
    all_to_all x3 -> x0, starting transfers between devices: 26.7 us -> none  [the longest x1 12.5 us: per_device(): lax.all_to_all(held_back.reshape(n_inner, per_inner, BLOCK, pair_width),...]
    reshape x5 -> x0, local copies, waits for them, and re-layouts: 18.4 us -> none  [the longest x1 8.56 us: per_device(): held_back.reshape(n_inner, per_inner, BLOCK, pair_width)]
    gather x4 -> x0, local copies, waits for them, and re-layouts: 14.1 us -> none  [the longest x1 4.2 us: per_device(): relayed = arrived.reshape(width_first, BLOCK, pair_width)[relay_from]]
  transfers between devices with their start and end apart: 4 -> 0, of which waited for: 4 -> 0; matrix products, arithmetic and copies ran while one was open for 13% -> 0% of each run, Pallas kernels for 0% -> 0%
where the time goes in v1:
time: 203 us
  Pallas kernels  191 us (94%)
  local copies, waits for them, and re-layouts  10.4 us (5%)
    pallas_call x1, Pallas kernels, give_back(): pl.pallas_call(return_kernel, out_shape=(jax.ShapeDtypeStruct((PARTS, 32,...  89.1 us
    pallas_call x1, Pallas kernels, fetch(): pl.pallas_call(fetch_kernel, out_shape=(jax.ShapeDtypeStruct((PARTS, 16,...  74.4 us
    pallas_call x1, Pallas kernels, attend(): pl.pallas_call(attend_kernel, out_shape=(jax.ShapeDtypeStruct((BLOCK, DIM...  21.5 us
    unnamed x31, local copies, waits for them, and re-layouts  10.4 us
    pallas_call x1, Pallas kernels, finish(): pl.pallas_call(final_kernel, out_shape=(jax.ShapeDtypeStruct((BLOCK, DIM)...  4.55 us

profile of v1, /device:TPU:1, one launch (start us, length us, event | category | flops | bytes accessed | tf_op | source)
XLA Modules:
  0.0 202.6 jit_solution(7284639360098924740)
XLA Ops:
  0.6 1.9 shard_map.110.tab
  2.5 0.7 copy.12.start
  3.3 0.0 copy-start.1
  3.3 0.0 copy-start.2
  3.3 0.0 copy-start.8
  3.3 0.0 copy-start.10
  3.3 74.4 %fetch.1 = (bf16[8,16,64,128]{3,2,1,0:T(8,128)(2,1)}, bf16[256,2048]{1,0:T(8,128)(2,1)}, bf16[256,2048]{1,0:T(8,128)(2,1)}) custom-call(s32[8,256]{1,0:T(8,128)} %shard_map.110.tab, bf16[256,2048]{1,0:T(8,128)(2,1)} %key.3, bf16[256,2048]{1,0:T(8,128)(2,1)} %value.3, bf16[256,2048]{1,0:T(8,128)(2,1)} %cot.3, bf16[2048,2048]{1,0:T(8,128)(2,1)} %weight.3), custom_call_target="tpu_custom_call" | custom-call | tf_op jit(solution)/shard_map/fetch/pallas_call | solution.py:254
  77.6 0.0 copy-done.1
  77.7 0.0 copy-done.2
  77.7 0.0 copy-done.8
  77.7 0.0 copy-done.10
  77.7 0.0 copy-start.9
  77.7 1.2 copy-done.9
  78.9 21.5 %attend.1 = (bf16[256,2048]{1,0:T(8,128)(2,1)S(1)}, bf16[16,4,2,16,256]{4,3,2,1,0:T(8,128)(2,1)S(1)}, bf16[256,2048]{1,0:T(8,128)(2,1)}, f32[256,2048]{1,0:T(8,1...) custom-call(s32[8,256]{1,0:T(8,128)S(1)} %copy-done.10, s32[16,1]{1,0:T(8,128)S(1)} %copy.12.start, ...), custom_call_target="tpu_custom_call" | custom-call | tf_op jit(solution)/shard_map/attend/pallas_call | solution.py:316
  100.4 0.0 copy-start.3
  100.4 1.3 copy-done.3
  101.7 0.0 copy-start.4
  101.7 1.3 copy-done.4
  103.1 0.0 copy-start.6
  103.1 1.0 copy-done.6
  104.0 0.0 copy-start.7
  104.0 1.0 copy-done.7
  105.0 89.1 %give_back.1 = (bf16[8,32,64,128]{3,2,1,0:T(8,128)(2,1)}, bf16[256,2048]{1,0:T(8,128)(2,1)}, f32[16,2048]{1,0:T(8,128)}) custom-call(s32[8,256]{1,0:T(8,128)} %shard_map.110.tab, bf16[8,16,64,128]{3,2,1,0:T(8,128)(2,1)} %copy-done.3, bf16[256,2048]{1,0:T(8,128)(2,1)} %copy-done.6, bf16[16,4,2,16,256]{4,3,2,1,0:T(8,128)(2,1)} %copy-done.7, ...), custom_call_target="tpu_custom_call" | custom-call | tf_op jit(solution)/shard_map/give_back/pallas_call | solution.py:522
  194.1 0.0 copy-done.5
  194.2 0.0 copy-done.11
  194.2 0.0 copy-start
  194.2 2.2 %copy-done = bf16[8,32,64,128]{3,2,1,0:T(8,128)(2,1)S(1)} copy-done((bf16[8,32,64,128]{3,2,1,0:T(8,128)(2,1)S(1)}, bf16[8,32,64,128]{3,2,1,0:T(8,128)(2,1)}, u32[]{:S(2)}) %copy-start) | copy-done | bytes 4194328
  196.4 4.5 %finish.1 = (bf16[256,2048]{1,0:T(8,128)(2,1)}, bf16[256,2048]{1,0:T(8,128)(2,1)}) custom-call(s32[8,256]{1,0:T(8,128)S(1)} %copy-done.11, bf16[8,32,64,128]{3,2,1,0:T(8,128)(2,1)S(1)} %copy-done, bf16[8,32,64,128]{3,2,1,0:T(8,128)(2,1)S(1)} %copy-done, f32[256,2048]{1,0:T(8,128)S(1)} %get-tuple-element.28.own_k, f32[256,2048]{1,0:T(8,128)S(1)} %copy-done.5), custom_call_target="tpu_custom_call" | custom-call | tf_op jit(solution)/shard_map/finish/pallas_call | solution.py:572
  200.9 0.0 copy-done.12
  200.9 1.0 copy.15
  201.9 0.0 copy-done.13
  201.9 0.7 copy.16
  (4 shorter events, 0.0 us)
Async XLA Ops:
  3.3 74.4 %copy-start.1 = (bf16[256,2048]{1,0:T(8,128)(2,1)S(1)}, bf16[256,2048]{1,0:T(8,128)(2,1)}, u32[]{:S(2)}) copy-start(bf16[256,2048]{1,0:T(8,128)(2,1)} %key.3) | copy-start | bytes 3145732
  3.3 74.4 %copy-start.2 = (bf16[256,2048]{1,0:T(8,128)(2,1)S(1)}, bf16[256,2048]{1,0:T(8,128)(2,1)}, u32[]{:S(2)}) copy-start(bf16[256,2048]{1,0:T(8,128)(2,1)} %value.3) | copy-start | bytes 3145732
  3.3 74.4 %copy-start.8 = (bf16[256,2048]{1,0:T(8,128)(2,1)S(1)}, bf16[256,2048]{1,0:T(8,128)(2,1)}, u32[]{:S(2)}) copy-start(bf16[256,2048]{1,0:T(8,128)(2,1)} %query.1) | copy-start | bytes 3145732
  3.3 74.4 %copy-start.10 = (s32[8,256]{1,0:T(8,128)S(1)}, s32[8,256]{1,0:T(8,128)}, u32[]{:S(2)}) copy-start(s32[8,256]{1,0:T(8,128)} %shard_map.110.tab) | copy-start | bytes 24580
  77.7 1.2 copy-start.9
  100.4 1.4 copy-start.3
  101.7 1.4 copy-start.4
  103.1 1.0 copy-start.6
  104.0 1.0 copy-start.7
  105.0 89.1 %copy-start.5 = (f32[256,2048]{1,0:T(8,128)S(1)}, f32[256,2048]{1,0:T(8,128)}, u32[]{:S(2)}) copy-start(f32[256,2048]{1,0:T(8,128)} %copy-done.4) | copy-start | bytes 6291460
  105.0 89.1 %copy-start.11 = (s32[8,256]{1,0:T(8,128)S(1)}, s32[8,256]{1,0:T(8,128)}, u32[]{:S(2)}) copy-start(s32[8,256]{1,0:T(8,128)} %shard_map.110.tab) | copy-start | bytes 24580
  194.2 2.2 %copy-start = (bf16[8,32,64,128]{3,2,1,0:T(8,128)(2,1)S(1)}, bf16[8,32,64,128]{3,2,1,0:T(8,128)(2,1)}, u32[]{:S(2)}) copy-start(bf16[8,32,64,128]{3,2,1,0:T(8,128)(2,1)} %get-tuple-element.27.back_k.back_v) | copy-start | bytes 12582916
  196.4 4.6 %copy-start.12 = (bf16[256,2048]{1,0:T(8,128)(2,1)S(1)}, bf16[256,2048]{1,0:T(8,128)(2,1)}, u32[]{:S(2)}) copy-start(bf16[256,2048]{1,0:T(8,128)(2,1)} %get-tuple-element.38) | copy-start | bytes 3145732
  200.9 1.0 copy-start.13

commit v2 on v1

--- a/solution.py
+++ b/solution.py
@@ -15,6 +15,12 @@
 HALF = PARTS // 2
 ROWS = BLOCK // HALF
 AHEAD = 2
+UNROLL = 4
+TWIN = 4
+EARLY = 4
+TILES = 8
+LATE = 7
+WHEN = ((7, 9), (6, 7), (6, 7))
 SCALE = 1.0 / math.sqrt(DH)
 MESH = pl.DeviceIdType.MESH
 STREAMS = ((0, 1024, "yzx"), (1024, 512, "xyz"), (1536, 512, "zxy"))
@@ -166,8 +172,8 @@
             zs[p, n - 4] = piece(n)
             return _
 
-        lax.fori_loop(0, 4, own, 0)
-        lax.fori_loop(4, 32, other, 0)
+        lax.fori_loop(0, 4, own, 0, unroll=4)
+        lax.fori_loop(4, 32, other, 0, unroll=UNROLL)
 
     def send_z(p):
         for j in range(1, 8):
@@ -187,13 +193,13 @@
             xs[p, n - 8] = zr[p][tab[0, T_X + n]]
             return _
 
-        lax.fori_loop(8, 32, other, 0)
+        lax.fori_loop(8, 32, other, 0, unroll=UNROLL)
         for d in range(1, 4):
             send(
                 xs.at[p, pl.ds((d - 1) * 8, 8)], xr[p].at[pl.ds(d * 8, 8)],
                 xss.at[p], xrs.at[p], step_x(pos, d),
             )
-        lax.fori_loop(0, 8, own, 0)
+        lax.fori_loop(0, 8, own, 0, unroll=UNROLL)
 
     def pass_y(p):
         settle(xr[p].at[pl.ds(8, 24)], xrs.at[p])
@@ -202,7 +208,7 @@
             ys[p, n] = xr[p][tab[0, T_Y + n]]
             return _
 
-        lax.fori_loop(0, 16, each, 0)
+        lax.fori_loop(0, 16, each, 0, unroll=UNROLL)
         for d in range(1, 4):
             send(
                 ys.at[p, pl.ds(d * 4, 4)], landed.at[p, pl.ds(d * 4, 4)],
@@ -211,6 +217,12 @@
         pltpu.make_async_copy(
             ys.at[p, pl.ds(0, 4)], landed.at[p, pl.ds(0, 4)], ysl.at[p]
         ).start()
+
+    def grad_tile(c):
+        cols = pl.ds(c * 256, 256)
+        grad[:, cols] = lax.dot_general(
+            cot[...], wbuf[cols, :], NT, preferred_element_type=F32
+        ).astype(BF16)
 
     gather_z(0)
     greet(pos)
@@ -219,24 +231,18 @@
         gather_z(p)
         send_z(p)
     send(cot, cot_other, cs, cr, step_z(pos, 0, 1))
-    for p in range(AHEAD, PARTS):
-        gather_z(p)
-    load_w.wait()
-
-    def grad_tile(c, _):
-        cols = pl.ds(pl.multiple_of(c * 256, 256), 256)
-        grad[:, cols] = lax.dot_general(
-            cot[...], wbuf[cols, :], NT, preferred_element_type=F32
-        ).astype(BF16)
-        return _
-
-    lax.fori_loop(0, 8, grad_tile, 0)
     for p in range(PARTS):
+        if p + AHEAD < PARTS:
+            gather_z(p + AHEAD)
+            send_z(p + AHEAD)
         pass_x(p)
-        if p + AHEAD < PARTS:
-            send_z(p + AHEAD)
         if p >= 1:
             pass_y(p - 1)
+        if p == 0:
+            load_w.wait()
+        for c in range(8):
+            if c * PARTS // 8 == p:
+                grad_tile(c)
     pass_y(PARTS - 1)
     for p in range(PARTS):
         settle(landed.at[p, pl.ds(4, 12)], yrs.at[p])
@@ -276,64 +282,6 @@
     )(tab, key, value, cot, weight)
 
 
-def attend_kernel(
-    tab, start, query, key, value, grad, landed,
-    att, att_t, grad_q, own_k, own_v, terms,
-):
-    h = pl.program_id(0)
-    q, g = query[...], grad[...]
-    keys = jnp.concatenate([key[...], landed[:HALF, 0].reshape(BLOCK, DH)], axis=0)
-    values = jnp.concatenate([value[...], landed[HALF:, 0].reshape(BLOCK, DH)], axis=0)
-    scores = lax.dot_general(q, keys, NT, preferred_element_type=F32) * SCALE
-    spot = lax.broadcasted_iota(jnp.int32, scores.shape, 1)
-    seen = (spot >= BLOCK) | (spot >= start[h, 0])
-    scores = jnp.where(seen, scores, -jnp.inf)
-    e = jnp.exp(scores - jnp.max(scores, axis=1, keepdims=True))
-    probs = e * (1.0 / jnp.sum(e, axis=1, keepdims=True))
-    probs_b = probs.astype(BF16)
-    a32 = jnp.dot(probs_b, values, preferred_element_type=F32)
-    a = a32.astype(BF16)
-    att[...] = a
-    att_t[...] = a.astype(F32).T.astype(BF16).reshape(1, 4, 2, 16, BLOCK)
-    delta = jnp.sum(g.astype(F32) * a.astype(F32), axis=1, keepdims=True)
-    pg = lax.dot_general(g, values, NT, preferred_element_type=F32)
-    ds = (probs * (pg - delta)).astype(BF16)
-    grad_q[...] = (jnp.dot(ds, keys, preferred_element_type=F32) * SCALE).astype(BF16)
-    kt = lax.dot_general(ds, q, TN, preferred_element_type=F32) * SCALE
-    vt = lax.dot_general(probs_b, g, TN, preferred_element_type=F32)
-    own_k[...] = kt[:BLOCK]
-    own_v[...] = vt[:BLOCK]
-    terms[:HALF, 0] = kt[BLOCK:].astype(BF16).reshape(HALF, ROWS, DH)
-    terms[HALF:, 0] = vt[BLOCK:].astype(BF16).reshape(HALF, ROWS, DH)
-
-
-def attend(tab, start, query, key, value, grad, landed):
-    head = pl.BlockSpec((BLOCK, DH), lambda h, tab, start: (0, h))
-    slot = pl.BlockSpec(
-        (PARTS, 1, ROWS, DH), lambda h, tab, start: (0, tab[0, T_SLOT + h], 0, 0)
-    )
-    turned = pl.BlockSpec((1, 4, 2, 16, BLOCK), lambda h, tab, start: (h, 0, 0, 0, 0))
-    return pl.pallas_call(
-        attend_kernel,
-        out_shape=(
-            jax.ShapeDtypeStruct((BLOCK, DIM), BF16),
-            jax.ShapeDtypeStruct((HEADS, 4, 2, 16, BLOCK), BF16),
-            jax.ShapeDtypeStruct((BLOCK, DIM), BF16),
-            jax.ShapeDtypeStruct((BLOCK, DIM), F32),
-            jax.ShapeDtypeStruct((BLOCK, DIM), F32),
-            jax.ShapeDtypeStruct((PARTS, 16, ROWS, DH), BF16),
-        ),
-        grid_spec=pltpu.PrefetchScalarGridSpec(
-            num_scalar_prefetch=2,
-            grid=(HEADS,),
-            in_specs=[head, head, head, head, slot],
-            out_specs=[head, turned, head, head, head, slot],
-        ),
-        compiler_params=pltpu.CompilerParams(vmem_limit_bytes=40 << 20),
-        name="attend",
-    )(tab, start, query, key, value, grad, landed)
-
-
 AXES = "xyz"
 
 
@@ -343,15 +291,16 @@
     return tuple(spot[: len(order)])
 
 
-def return_kernel(
-    tab, terms, att, att_t, cot, cot_other, weight,
-    back, layer, wgrad, *scratch,
+def attend_kernel(
+    tab, start, query, key, value, grad, landed, cot_in, cot_other_in, weight,
+    back, layer_out, wgrad, grad_q_out, own_k_out, own_v_out, *scratch
 ):
     xb, scratch = scratch[:PARTS], scratch[PARTS:]
     (
-    wbuf, at_other, yb, zs, g0, g1, g2, r10, r11, r12, s10, s11, s12,
-    r20, r21, r22, s20, s21, s22, r30, r31, r32,
-    yss, yrs, ysl, xss, xrs, zss, zrs, zsl, as_, ar, ws, rs, rr,
+        q_in, k_in, v_in, g_in, f_in, cot, cot_other, wbuf,
+        att, att_t, at_other, pbuf, grad_q, own_k, own_v, layer, terms, ys, yb, zs,
+        g0, g1, g2, r10, r11, r12, s10, s11, s12, r20, r21, r22, s20, s21, s22, r30, r31, r32,
+        yss, yrs, xss, xrs, zss, zrs, zsl, as_, ar, ins, outs, rs, rr,
     ) = scratch
     pos = here()
     coord = dict(zip(AXES, pos[:3]))
@@ -359,22 +308,86 @@
     go = {"x": step_x, "y": step_y, "z": lambda pos, d: step_z(pos, d, 0)}
     g, r1, s1 = (g0, g1, g2), (r10, r11, r12), (s10, s11, s12)
     r2, s2, r3 = (r20, r21, r22), (s20, s21, s22), (r30, r31, r32)
-    load_w = pltpu.make_async_copy(weight, wbuf, ws)
-    load_w.start()
+    loads = [
+        pltpu.make_async_copy(src, dst, ins.at[n])
+        for n, (src, dst) in enumerate(
+            (
+                (query, q_in), (key, k_in), (landed, f_in), (value, v_in), (grad, g_in),
+                (cot_in, cot), (cot_other_in, cot_other), (weight, wbuf),
+            )
+        )
+    ]
+    for load in loads:
+        load.start()
     greet(pos)
+
+    def fetched(h, first):
+        slot = tab[0, T_SLOT + h]
+        return jnp.concatenate([f_in[p, slot] for p in range(first, first + HALF)], axis=0)
+
+    def forward(h, _):
+        cols = pl.ds(pl.multiple_of(h * DH, DH), DH)
+        qh = q_in[:, cols]
+        own = lax.dot_general(qh, k_in[:, cols], NT, preferred_element_type=F32) * SCALE
+        spot = lax.broadcasted_iota(jnp.int32, own.shape, 1)
+        own = jnp.where(spot >= start[h, 0], own, -jnp.inf)
+        far = lax.dot_general(qh, fetched(h, 0), NT, preferred_element_type=F32) * SCALE
+        top = jnp.max(jnp.maximum(own, far), axis=1, keepdims=True)
+        own, far = jnp.exp(own - top), jnp.exp(far - top)
+        share = 1.0 / jnp.sum(own + far, axis=1, keepdims=True)
+        own, far = own * share, far * share
+        pbuf[h, 0] = own
+        pbuf[h, 1] = far
+        a = jnp.dot(own.astype(BF16), v_in[:, cols], preferred_element_type=F32)
+        a += jnp.dot(far.astype(BF16), fetched(h, HALF), preferred_element_type=F32)
+        a = a.astype(BF16)
+        att[:, cols] = a
+        att_t[h] = a.astype(F32).T.astype(BF16).reshape(4, 2, 16, BLOCK)
+        return _
+
+    def backward(h, _):
+        cols = pl.ds(pl.multiple_of(h * DH, DH), DH)
+        gh, qh, probs = g_in[:, cols], q_in[:, cols], pbuf[h, 1]
+        delta = jnp.sum(gh.astype(F32) * att[:, cols].astype(F32), axis=1, keepdims=True)
+        pg = lax.dot_general(gh, fetched(h, HALF), NT, preferred_element_type=F32)
+        ds = (probs * (pg - delta)).astype(BF16)
+        kt = lax.dot_general(ds, qh, TN, preferred_element_type=F32) * SCALE
+        vt = lax.dot_general(probs.astype(BF16), gh, TN, preferred_element_type=F32)
+        pbuf[h, 1] = ds.astype(F32)
+        for p in range(HALF):
+            rows = slice(p * ROWS, (p + 1) * ROWS)
+            terms[p, h] = kt[rows].astype(BF16)
+            terms[p + HALF, h] = vt[rows].astype(BF16)
+        return _
+
+    def backward_own(h, _):
+        cols = pl.ds(pl.multiple_of(h * DH, DH), DH)
+        gh, qh, kh, probs = g_in[:, cols], q_in[:, cols], k_in[:, cols], pbuf[h, 0]
+        delta = jnp.sum(gh.astype(F32) * att[:, cols].astype(F32), axis=1, keepdims=True)
+        pg = lax.dot_general(gh, v_in[:, cols], NT, preferred_element_type=F32)
+        ds = (probs * (pg - delta)).astype(BF16)
+        gq = jnp.dot(ds, kh, preferred_element_type=F32)
+        gq += jnp.dot(pbuf[h, 1].astype(BF16), fetched(h, 0), preferred_element_type=F32)
+        grad_q[:, cols] = (gq * SCALE).astype(BF16)
+        kt = lax.dot_general(ds, qh, TN, preferred_element_type=F32) * SCALE
+        vt = lax.dot_general(probs.astype(BF16), gh, TN, preferred_element_type=F32)
+        own_k[h] = kt.astype(BF16)
+        own_v[h] = vt.astype(BF16)
+        return _
+
+    for load in loads[:4]:
+        load.wait()
+    lax.fori_loop(0, HEADS, forward, 0, unroll=TWIN)
     send(att_t.at[:, :, 1 - k], at_other, as_, ar, step_z(pos, 0, 1))
-    for p in range(PARTS):
-        for d in range(1, 4):
-            send(
-                terms.at[p, pl.ds(d * 4, 4)], yb.at[p, d], yss.at[p], yrs.at[p],
-                step_y(pos, 4 - d),
-            )
-        pltpu.make_async_copy(terms.at[p, pl.ds(0, 4)], yb.at[p, 0], ysl.at[p]).start()
+    for load in loads[4:7]:
+        load.wait()
+    lax.fori_loop(0, EARLY, backward, 0, unroll=TWIN)
     settle(at_other, ar)
 
-    for n, (first, width, order) in enumerate(STREAMS):
-
-        def tile(m, c, n=n, first=first):
+    def partial(n):
+        first, width, _ = STREAMS[n]
+
+        def tile(m, c):
             cols = pl.ds(pl.multiple_of(first + c * 256, 256), 256)
             mine = att_t[pl.ds(m * 4, 4), :, k].reshape(256, BLOCK)
             theirs = at_other[pl.ds(m * 4, 4)].reshape(256, BLOCK)
@@ -385,21 +398,44 @@
             for i in range(4):
                 g[n][(m // 2) * 2 + i % 2, (m % 2) * 2 + i // 2, :, :, out] = t[i]
 
-        def tiles(i, _, tile=tile, n=n, first=first):
+        def tiles(i, _):
             tile(i % 4, i // 4)
             return _
 
-        lax.fori_loop(0, 4 * (width // 256), tiles, 0)
-        a = order[0]
+        lax.fori_loop(0, 4 * (width // 256), tiles, 0, unroll=TILES)
+
+    def send_one(n):
+        a = STREAMS[n][2][0]
         for d in range(1, 4):
             send(
                 g[n].at[pick(AXES, a, (coord[a] + d) % 4)], r1[n].at[d - 1],
                 rs.at[n, 0], rr.at[n, 0], go[a](pos, d),
             )
 
+    for n in (2, 1):
+        partial(n)
+        send_one(n)
+    lax.fori_loop(EARLY, HEADS, backward, 0, unroll=TWIN)
+
+    def return_y(p):
+        def own(n, _):
+            yb[p, 0, n] = terms[p, tab[0, T_HEAD + n]]
+            return _
+
+        def other(n, _):
+            ys[p, n - 4] = terms[p, tab[0, T_HEAD + n]]
+            return _
+
+        lax.fori_loop(4, 16, other, 0, unroll=4)
+        for d in range(1, 4):
+            send(
+                ys.at[p, pl.ds(d * 4 - 4, 4)], yb.at[p, d], yss.at[p], yrs.at[p],
+                step_y(pos, 4 - d),
+            )
+        lax.fori_loop(0, 4, own, 0, unroll=4)
+
     def return_x(p):
         settle(yb.at[p, pl.ds(1, 3)], yrs.at[p])
-        settle(yb.at[p, 0], ysl.at[p])
         for d in range(4):
             half = ((pos[0] + 4 - d) % 4) // 2
             src = yb.at[p, :, pl.ds(half * 2, 2)]
@@ -416,7 +452,7 @@
             zs[p, n] = xb[p][e // 8, (e // 2) % 4, e % 2]
             return _
 
-        lax.fori_loop(0, 32, each, 0)
+        lax.fori_loop(0, 32, each, 0, unroll=UNROLL)
         for j in range(1, 8):
             send(
                 zs.at[p, pl.ds(j * 4, 4)], back.at[p, pl.ds(j * 4, 4)],
@@ -479,8 +515,6 @@
             t += r3[n][d].astype(F32)
         wgrad[:, pl.ds(first, width)] = t * (1.0 / math.sqrt(BLOCK * 128))
 
-    load_w.wait()
-
     def layer_tile(c, _):
         cols = pl.ds(pl.multiple_of(c * 256, 256), 256)
         layer[:, cols] = jnp.dot(
@@ -488,87 +522,121 @@
         ).astype(BF16)
         return _
 
+    stores = [
+        pltpu.make_async_copy(src, dst, outs.at[n])
+        for n, (src, dst) in enumerate(
+            ((grad_q, grad_q_out), (own_k, own_k_out), (own_v, own_v_out), (layer, layer_out))
+        )
+    ]
+    for p in range(PARTS):
+        return_y(p)
+        if p == LATE:
+            partial(0)
+    send_one(0)
+    each = HEADS // PARTS
     for p in range(PARTS):
         return_x(p)
-        if p == 0:
-            lax.fori_loop(0, 8, layer_tile, 0)
         if p >= 1:
             return_z(p - 1)
-        if p == 4:
+        if p == 1:
+            loads[7].wait()
+            lax.fori_loop(0, 8, layer_tile, 0)
+            stores[3].start()
+        lax.fori_loop(p * each, (p + 1) * each, backward_own, 0, unroll=each)
+        for level, step in enumerate((sum_one, sum_two)):
             for n in range(3):
-                sum_one(n)
-        if p == 6:
-            for n in range(3):
-                sum_two(n)
+                if WHEN[n][level] == p:
+                    step(n)
+    for store in stores[:3]:
+        store.start()
     return_z(PARTS - 1)
-    for n in range(3):
+    for n in (1, 2):
         sum_three(n)
+    sum_two(0)
+    sum_three(0)
     for p in range(PARTS):
         settle(back.at[p, pl.ds(4, 28)], zrs.at[p])
         settle(back.at[p, pl.ds(0, 4)], zsl.at[p])
         settle(zs.at[p, pl.ds(4, 28)], zss.at[p])
         settle(xb[p].at[pl.ds(1, 3)], xss.at[p])
-        settle(yb.at[p, pl.ds(1, 3)], yss.at[p])
+        settle(ys.at[p], yss.at[p])
     settle(at_other, as_)
-
-
-def give_back(tab, terms, att, att_t, cot, cot_other, weight):
+    for store in stores:
+        store.wait()
+
+
+def attend(tab, start, query, key, value, grad, landed, cot, cot_other, weight):
     slot = (ROWS, DH)
+    tokens = (BLOCK, DIM)
     widths = [w for _, w, _ in STREAMS]
     per_stream = [
         [pltpu.VMEM((*lead, 16, w), BF16) for w in widths]
         for lead in ((4, 4, 4), (3, 4, 4), (4, 4), (3, 4), (4,), (3,))
     ]
     return pl.pallas_call(
-        return_kernel,
+        attend_kernel,
         out_shape=(
             jax.ShapeDtypeStruct((PARTS, 32, *slot), BF16),
-            jax.ShapeDtypeStruct((BLOCK, DIM), BF16),
+            jax.ShapeDtypeStruct(tokens, BF16),
             jax.ShapeDtypeStruct((16, DIM), F32),
+            jax.ShapeDtypeStruct(tokens, BF16),
+            jax.ShapeDtypeStruct((HEADS, BLOCK, DH), BF16),
+            jax.ShapeDtypeStruct((HEADS, BLOCK, DH), BF16),
         ),
-        in_specs=[SMEM, VMEM, VMEM, VMEM, VMEM, VMEM, ANY],
-        out_specs=(VMEM, VMEM, VMEM),
+        in_specs=[SMEM, SMEM, *[ANY] * 8],
+        out_specs=(ANY, ANY, VMEM, ANY, ANY, ANY),
         scratch_shapes=[
             *[pltpu.VMEM((4, 4, 2, *slot), BF16)] * PARTS,
+            *[pltpu.VMEM(tokens, BF16)] * 4,
+            pltpu.VMEM((PARTS, 16, *slot), BF16),
+            *[pltpu.VMEM(tokens, BF16)] * 2,
             pltpu.VMEM((DIM, DIM), BF16),
+            pltpu.VMEM(tokens, BF16),
+            pltpu.VMEM((HEADS, 4, 2, 16, BLOCK), BF16),
             pltpu.VMEM((HEADS, 4, 16, BLOCK), BF16),
+            pltpu.VMEM((HEADS, 2, BLOCK, BLOCK), F32),
+            pltpu.VMEM(tokens, BF16),
+            pltpu.VMEM((HEADS, BLOCK, DH), BF16),
+            pltpu.VMEM((HEADS, BLOCK, DH), BF16),
+            pltpu.VMEM(tokens, BF16),
+            pltpu.VMEM((PARTS, 16, *slot), BF16),
+            pltpu.VMEM((PARTS, 12, *slot), BF16),
             pltpu.VMEM((PARTS, 4, 4, *slot), BF16),
             pltpu.VMEM((PARTS, 32, *slot), BF16),
             *[buf for level in per_stream for buf in level],
-            *[pltpu.SemaphoreType.DMA((PARTS,))] * 8,
-            *[pltpu.SemaphoreType.DMA] * 3,
+            *[pltpu.SemaphoreType.DMA((PARTS,))] * 7,
+            *[pltpu.SemaphoreType.DMA] * 2,
+            pltpu.SemaphoreType.DMA((8,)),
+            pltpu.SemaphoreType.DMA((4,)),
             pltpu.SemaphoreType.DMA((3, 3)),
             pltpu.SemaphoreType.DMA((3, 3)),
         ],
         compiler_params=pltpu.CompilerParams(
-            collective_id=1, has_side_effects=True, vmem_limit_bytes=58 << 20
+            collective_id=1, has_side_effects=True, vmem_limit_bytes=62 << 20
         ),
-        name="give_back",
-    )(tab, terms, att, att_t, cot, cot_other, weight)
+        name="attend",
+    )(tab, start, query, key, value, grad, landed, cot, cot_other, weight)
 
 
 def final_kernel(tab, back_k, back_v, own_k, own_v, grad_k, grad_v, sum_k, sum_v):
-    sum_k[...] = own_k[...]
-    sum_v[...] = own_v[...]
+    sum_k[1:] = own_k[...].astype(F32)
+    sum_v[1:] = own_v[...].astype(F32)
 
     def add(n, _):
         h = tab[0, T_USED + n]
-
-        @pl.when(h > 0)
-        def _add():
-            cols = pl.ds(pl.multiple_of((h - 1) * DH, DH), DH)
-            sum_k[:, cols] += back_k[0, n].astype(F32)
-            sum_v[:, cols] += back_v[0, n].astype(F32)
-
+        sum_k[h] += back_k[0, n].astype(F32)
+        sum_v[h] += back_v[0, n].astype(F32)
         return _
 
-    lax.fori_loop(0, 32, add, 0)
-    grad_k[...] = sum_k[...].astype(BF16)
-    grad_v[...] = sum_v[...].astype(BF16)
+    lax.fori_loop(0, 32, add, 0, unroll=4)
+    for h in range(HEADS):
+        grad_k[:, h * DH : (h + 1) * DH] = sum_k[1 + h].astype(BF16)
+        grad_v[:, h * DH : (h + 1) * DH] = sum_v[1 + h].astype(BF16)
 
 
 def finish(tab, back, own_k, own_v):
     rows = pl.BlockSpec((ROWS, DIM), lambda p, tab: (p, 0))
+    own = pl.BlockSpec((HEADS, ROWS, DH), lambda p, tab: (0, p, 0))
     return pl.pallas_call(
         final_kernel,
         out_shape=(
@@ -581,13 +649,13 @@
             in_specs=[
                 pl.BlockSpec((1, 32, ROWS, DH), lambda p, tab: (p, 0, 0, 0)),
                 pl.BlockSpec((1, 32, ROWS, DH), lambda p, tab: (p + HALF, 0, 0, 0)),
-                rows,
-                rows,
+                own,
+                own,
             ],
             out_specs=[rows, rows],
-            scratch_shapes=[pltpu.VMEM((ROWS, DIM), F32)] * 2,
+            scratch_shapes=[pltpu.VMEM((HEADS + 1, ROWS, DH), F32)] * 2,
         ),
-        compiler_params=pltpu.CompilerParams(vmem_limit_bytes=40 << 20),
+        compiler_params=pltpu.CompilerParams(vmem_limit_bytes=60 << 20),
         name="finish",
     )(tab, back, back, own_k, own_v)
 
@@ -597,10 +665,10 @@
 ):
     tab = make_tables(sorted_blocks)
     landed, grad, cot_other = fetch(tab, key_rows, value_rows, cotangent, out_weight)
-    att, att_t, grad_q, own_k, own_v, terms = attend(
-        tab, window_start, query_rows, key_rows, value_rows, grad, landed
+    back, layer, wgrad, grad_q, own_k, own_v = attend(
+        tab, window_start, query_rows, key_rows, value_rows, grad, landed,
+        cotangent, cot_other, out_weight,
     )
-    back, layer, wgrad = give_back(tab, terms, att, att_t, cotangent, cot_other, out_weight)
     grad_k, grad_v = finish(tab, back, own_k, own_v)
     return layer, grad_q, grad_k, grad_v, wgrad
 

time: 203 us -> 178 us (0.88)
  Pallas kernels: 191 us -> 173 us
  local copies, waits for them, and re-layouts: 10.4 us -> 3.94 us
    pallas_call x2 -> x1, Pallas kernels: 111 us -> 91.1 us  [attend(): pl.pallas_call(attend_kernel, out_shape=(jax.ShapeDtypeStruct((PARTS, 32,...]
    unnamed x31 -> x10, local copies, waits for them, and re-layouts: 10.4 us -> 3.94 us
where the time goes in v2:
time: 178 us
  Pallas kernels  173 us (97%)
  local copies, waits for them, and re-layouts  3.94 us (2%)
    pallas_call x1, Pallas kernels, attend(): pl.pallas_call(attend_kernel, out_shape=(jax.ShapeDtypeStruct((PARTS, 32,...  91.1 us
    pallas_call x1, Pallas kernels, fetch(): pl.pallas_call(fetch_kernel, out_shape=(jax.ShapeDtypeStruct((PARTS, 16,...  73.9 us
    pallas_call x1, Pallas kernels, finish(): pl.pallas_call(final_kernel, out_shape=(jax.ShapeDtypeStruct((BLOCK, DIM)...  6.27 us
    unnamed x10, local copies, waits for them, and re-layouts  3.94 us

profile of v2, /device:TPU:1, one launch (start us, length us, event | category | flops | bytes accessed | tf_op | source)
XLA Modules:
  0.0 177.8 jit_solution(9221872263366821732)
XLA Ops:
  0.6 1.9 %shard_map.110.tab = s32[8,256]{1,0:T(8,128)} custom-call(s32[16,128]{1,0:T(8,128)} %src_ref.1), custom_call_target="tpu_custom_call" | custom-call | tf_op jit(solution)/shard_map/pallas_call | solution.py:140
  2.5 1.3 copy.12.start
  3.9 73.9 %fetch.1 = (bf16[8,16,64,128]{3,2,1,0:T(8,128)(2,1)}, bf16[256,2048]{1,0:T(8,128)(2,1)}, bf16[256,2048]{1,0:T(8,128)(2,1)}) custom-call(s32[8,256]{1,0:T(8,128)} %shard_map.110.tab, bf16[256,2048]{1,0:T(8,128)(2,1)} %key.3, bf16[256,2048]{1,0:T(8,128)(2,1)} %value.3, bf16[256,2048]{1,0:T(8,128)(2,1)} %cot_in.1, bf16[2048,2048]{1,0:T(8,128)(2,1)} %weight.3), custom_call_target="tpu_custom_call" | custom-call | tf_op jit(solution)/shard_map/fetch/pallas_call | solution.py:260
  77.8 91.1 %attend.1 = (bf16[8,32,64,128]{3,2,1,0:T(8,128)(2,1)}, bf16[256,2048]{1,0:T(8,128)(2,1)}, f32[16,2048]{1,0:T(8,128)}, bf16[256,2048]{1,0:T(8,128)(2,1)}, bf16[16...) custom-call(s32[8,256]{1,0:T(8,128)} %shard_map.110.tab, s32[16,1]{1,0:T(8,128)} %copy.12.start, ...), custom_call_target="tpu_custom_call" | custom-call | tf_op jit(solution)/shard_map/attend/pallas_call | solution.py:576
  168.9 0.0 copy-start.1
  168.9 0.0 copy-start
  168.9 6.3 %finish.1 = (bf16[256,2048]{1,0:T(8,128)(2,1)}, bf16[256,2048]{1,0:T(8,128)(2,1)}) custom-call(s32[8,256]{1,0:T(8,128)} %shard_map.110.tab, bf16[8,32,64,128]{3,2,1,0:T(8,128)(2,1)} %get-tuple-element.21.back_k.back_v, bf16[8,32,64,128]{3,2,1,0:T(8,128)(2,1)} %get-tuple-element.21.back_k.back_v, bf16[16,256,128]{2,1,0:T(8,128)(2,1)} %get-tuple-element.22.own_k, ...), custom_call_target="tpu_custom_call" | custom-call | tf_op jit(solution)/shard_map/finish/pallas_call | solution.py:640
  175.2 0.0 copy-start.2
  175.2 0.0 copy-done.1
  175.2 1.0 copy.16
  176.2 0.0 copy-done
  176.2 1.0 copy.17
  177.1 0.0 copy-done.2
  177.1 0.7 copy.18
Async XLA Ops:
  168.9 6.3 %copy-start.1 = (bf16[256,2048]{1,0:T(8,128)(2,1)S(1)}, bf16[256,2048]{1,0:T(8,128)(2,1)}, u32[]{:S(2)}) copy-start(bf16[256,2048]{1,0:T(8,128)(2,1)} %get-tuple-element.32) | copy-start | bytes 3145732
  168.9 7.3 %copy-start = (bf16[256,2048]{1,0:T(8,128)(2,1)S(1)}, bf16[256,2048]{1,0:T(8,128)(2,1)}, u32[]{:S(2)}) copy-start(bf16[256,2048]{1,0:T(8,128)(2,1)} %get-tuple-element.33) | copy-start | bytes 3145732
  175.2 2.0 %copy-start.2 = (f32[16,2048]{1,0:T(8,128)S(1)}, f32[16,2048]{1,0:T(8,128)}, u32[]{:S(2)}) copy-start(f32[16,2048]{1,0:T(8,128)} %get-tuple-element.36) | copy-start | bytes 393220

commit v3 on v2

--- a/solution.py
+++ b/solution.py
@@ -17,6 +17,9 @@
 AHEAD = 2
 UNROLL = 4
 TWIN = 4
+GRAD = 4
+JOIN = 2
+PAIR = 4
 EARLY = 4
 TILES = 8
 LATE = 7
@@ -146,10 +149,11 @@
 
 
 def fetch_kernel(
-    tab, key, value, cot, weight, landed, grad, cot_other, *scratch
+    tab, key, value, cot, weight, landed, grad_out, cot_other, *scratch
 ):
     zr, xr, scratch = scratch[:PARTS], scratch[PARTS : 2 * PARTS], scratch[2 * PARTS :]
-    wbuf, kv, zs, xs, ys, zss, zrs, xss, xrs, yss, yrs, ysl, cs, cr, wsem = scratch
+    wbuf, grad, kv, zs, xs, ys, zss, zrs, xss, xrs, yss, yrs, ysl, cs, cr, wsem, gsem = scratch
+    store = pltpu.make_async_copy(grad, grad_out, gsem)
     pos = here()
     load_w = pltpu.make_async_copy(weight, wbuf, wsem)
     load_w.start()
@@ -238,11 +242,11 @@
         pass_x(p)
         if p >= 1:
             pass_y(p - 1)
-        if p == 0:
+        if p == GRAD:
             load_w.wait()
-        for c in range(8):
-            if c * PARTS // 8 == p:
+            for c in range(8):
                 grad_tile(c)
+            store.start()
     pass_y(PARTS - 1)
     for p in range(PARTS):
         settle(landed.at[p, pl.ds(4, 12)], yrs.at[p])
@@ -252,11 +256,12 @@
         settle(ys.at[p, pl.ds(4, 12)], yss.at[p])
     settle(cot_other, cr)
     settle(cot, cs)
+    store.wait()
 
 
 def fetch(tab, key, value, cot, weight):
     slot = (ROWS, DH)
-    sems = [pltpu.SemaphoreType.DMA((PARTS,))] * 7 + [pltpu.SemaphoreType.DMA] * 3
+    sems = [pltpu.SemaphoreType.DMA((PARTS,))] * 7 + [pltpu.SemaphoreType.DMA] * 4
     return pl.pallas_call(
         fetch_kernel,
         out_shape=(
@@ -265,10 +270,11 @@
             jax.ShapeDtypeStruct((BLOCK, DIM), BF16),
         ),
         in_specs=[SMEM, VMEM, VMEM, VMEM, ANY],
-        out_specs=(VMEM, VMEM, VMEM),
+        out_specs=(ANY, ANY, ANY),
         scratch_shapes=[
             *[pltpu.VMEM((32, *slot), BF16)] * (2 * PARTS),
             pltpu.VMEM((DIM, DIM), BF16),
+            pltpu.VMEM((BLOCK, DIM), BF16),
             pltpu.VMEM((PARTS, HEADS, *slot), BF16),
             pltpu.VMEM((PARTS, 28, *slot), BF16),
             pltpu.VMEM((PARTS, 24, *slot), BF16),
@@ -317,7 +323,7 @@
             )
         )
     ]
-    for load in loads:
+    for load in loads[:4]:
         load.start()
     greet(pos)
 
@@ -330,7 +336,7 @@
         qh = q_in[:, cols]
         own = lax.dot_general(qh, k_in[:, cols], NT, preferred_element_type=F32) * SCALE
         spot = lax.broadcasted_iota(jnp.int32, own.shape, 1)
-        own = jnp.where(spot >= start[h, 0], own, -jnp.inf)
+        own = jnp.where(spot >= start[0, h], own, -jnp.inf)
         far = lax.dot_general(qh, fetched(h, 0), NT, preferred_element_type=F32) * SCALE
         top = jnp.max(jnp.maximum(own, far), axis=1, keepdims=True)
         own, far = jnp.exp(own - top), jnp.exp(far - top)
@@ -377,7 +383,9 @@
 
     for load in loads[:4]:
         load.wait()
-    lax.fori_loop(0, HEADS, forward, 0, unroll=TWIN)
+    for load in loads[4:7]:
+        load.start()
+    lax.fori_loop(0, HEADS, forward, 0, unroll=PAIR)
     send(att_t.at[:, :, 1 - k], at_other, as_, ar, step_z(pos, 0, 1))
     for load in loads[4:7]:
         load.wait()
@@ -412,6 +420,7 @@
                 rs.at[n, 0], rr.at[n, 0], go[a](pos, d),
             )
 
+    loads[7].start()
     for n in (2, 1):
         partial(n)
         send_one(n)
@@ -618,46 +627,56 @@
     )(tab, start, query, key, value, grad, landed, cot, cot_other, weight)
 
 
-def final_kernel(tab, back_k, back_v, own_k, own_v, grad_k, grad_v, sum_k, sum_v):
-    sum_k[1:] = own_k[...].astype(F32)
-    sum_v[1:] = own_v[...].astype(F32)
-
-    def add(n, _):
+def final_kernel(
+    tab, back_k, back_v, own_k, own_v, layer, grad_q, wgrad,
+    grad_k, grad_v, layer_out, grad_q_out, wgrad_out, *sums
+):
+    layer_out[...] = layer[...]
+    grad_q_out[...] = grad_q[...]
+    wgrad_out[...] = wgrad[...]
+
+    parts = [(back, own, i) for i in range(JOIN) for back, own in ((back_k, own_k), (back_v, own_v))]
+    for total, (_, own, i) in zip(sums, parts):
+        total[1:] = own[:, i * ROWS : (i + 1) * ROWS].astype(F32)
+
+    def add(n, carry):
         h = tab[0, T_USED + n]
-        sum_k[h] += back_k[0, n].astype(F32)
-        sum_v[h] += back_v[0, n].astype(F32)
-        return _
+        for total, (back, _, i) in zip(sums, parts):
+            total[h] += back[i, n].astype(F32)
+        return carry
 
     lax.fori_loop(0, 32, add, 0, unroll=4)
     for h in range(HEADS):
-        grad_k[:, h * DH : (h + 1) * DH] = sum_k[1 + h].astype(BF16)
-        grad_v[:, h * DH : (h + 1) * DH] = sum_v[1 + h].astype(BF16)
-
-
-def finish(tab, back, own_k, own_v):
-    rows = pl.BlockSpec((ROWS, DIM), lambda p, tab: (p, 0))
-    own = pl.BlockSpec((HEADS, ROWS, DH), lambda p, tab: (0, p, 0))
+        for total, (back, _, i) in zip(sums, parts):
+            out = grad_k if back is back_k else grad_v
+            out[i * ROWS : (i + 1) * ROWS, h * DH : (h + 1) * DH] = total[1 + h].astype(BF16)
+
+
+def finish(tab, back, own_k, own_v, layer, grad_q, wgrad):
+    steps = HALF // JOIN
+    rows = pl.BlockSpec((ROWS * JOIN, DIM), lambda p, tab: (p, 0))
+    own = pl.BlockSpec((HEADS, ROWS * JOIN, DH), lambda p, tab: (0, p, 0))
+    whole = pl.BlockSpec((16, DIM), lambda p, tab: (0, 0))
+    tokens = jax.ShapeDtypeStruct((BLOCK, DIM), BF16)
     return pl.pallas_call(
         final_kernel,
-        out_shape=(
-            jax.ShapeDtypeStruct((BLOCK, DIM), BF16),
-            jax.ShapeDtypeStruct((BLOCK, DIM), BF16),
-        ),
+        out_shape=(tokens, tokens, tokens, tokens, jax.ShapeDtypeStruct((16, DIM), F32)),
         grid_spec=pltpu.PrefetchScalarGridSpec(
             num_scalar_prefetch=1,
-            grid=(HALF,),
+            grid=(steps,),
             in_specs=[
-                pl.BlockSpec((1, 32, ROWS, DH), lambda p, tab: (p, 0, 0, 0)),
-                pl.BlockSpec((1, 32, ROWS, DH), lambda p, tab: (p + HALF, 0, 0, 0)),
-                own,
-                own,
+                pl.BlockSpec((JOIN, 32, ROWS, DH), lambda p, tab: (p, 0, 0, 0)),
+                pl.BlockSpec((JOIN, 32, ROWS, DH), lambda p, tab: (p + steps, 0, 0, 0)),
+                own, own, rows, rows, whole,
             ],
-            out_specs=[rows, rows],
-            scratch_shapes=[pltpu.VMEM((HEADS + 1, ROWS, DH), F32)] * 2,
+            out_specs=[rows, rows, rows, rows, whole],
+            scratch_shapes=[
+                *[pltpu.VMEM((HEADS + 1, ROWS, DH), F32)] * (2 * JOIN),
+            ],
         ),
         compiler_params=pltpu.CompilerParams(vmem_limit_bytes=60 << 20),
         name="finish",
-    )(tab, back, back, own_k, own_v)
+    )(tab, back, back, own_k, own_v, layer, grad_q, wgrad)
 
 
 def per_device(
@@ -666,10 +685,12 @@
     tab = make_tables(sorted_blocks)
     landed, grad, cot_other = fetch(tab, key_rows, value_rows, cotangent, out_weight)
     back, layer, wgrad, grad_q, own_k, own_v = attend(
-        tab, window_start, query_rows, key_rows, value_rows, grad, landed,
+        tab, window_start.reshape(1, HEADS), query_rows, key_rows, value_rows, grad, landed,
         cotangent, cot_other, out_weight,
     )
-    grad_k, grad_v = finish(tab, back, own_k, own_v)
+    grad_k, grad_v, layer, grad_q, wgrad = finish(
+        tab, back, own_k, own_v, layer, grad_q, wgrad
+    )
     return layer, grad_q, grad_k, grad_v, wgrad
 
 

time: 178 us -> 173 us (0.972)
  local copies, waits for them, and re-layouts: 3.94 us -> 0 us
  Pallas kernels: 173 us -> 171 us
    unnamed x10 -> x0, local copies, waits for them, and re-layouts: 3.94 us -> none
    pallas_call x1, Pallas kernels: 73.9 us -> 72 us  [fetch(): pl.pallas_call(fetch_kernel, out_shape=(jax.ShapeDtypeStruct((PARTS, 16,...]
where the time goes in v3:
time: 173 us; the launch traced here: 172 us
  Pallas kernels  171 us (99%)
    pallas_call x1, Pallas kernels, attend(): pl.pallas_call(attend_kernel, out_shape=(jax.ShapeDtypeStruct((PARTS, 32,...  90.9 us
    pallas_call x1, Pallas kernels, fetch(): pl.pallas_call(fetch_kernel, out_shape=(jax.ShapeDtypeStruct((PARTS, 16,...  72 us
    pallas_call x1, Pallas kernels, finish(): pl.pallas_call(final_kernel, out_shape=(tokens, tokens, tokens, tokens, j...  6.26 us

profile of v3, /device:TPU:1, one launch (start us, length us, event | category | flops | bytes accessed | tf_op | source)
XLA Modules:
  0.0 171.9 jit_solution(13287472444816537189)
XLA Ops:
  0.6 1.9 %shard_map.110.tab = s32[8,256]{1,0:T(8,128)} custom-call(s32[16,128]{1,0:T(8,128)} %src_ref.1), custom_call_target="tpu_custom_call" | custom-call | tf_op jit(solution)/shard_map/pallas_call | solution.py:143
  2.5 72.0 %fetch.1 = (bf16[8,16,64,128]{3,2,1,0:T(8,128)(2,1)}, bf16[256,2048]{1,0:T(8,128)(2,1)}, bf16[256,2048]{1,0:T(8,128)(2,1)}) custom-call(s32[8,256]{1,0:T(8,128)} %shard_map.110.tab, bf16[256,2048]{1,0:T(8,128)(2,1)} %key.3, bf16[256,2048]{1,0:T(8,128)(2,1)} %value.3, bf16[256,2048]{1,0:T(8,128)(2,1)} %cot_in.1, bf16[2048,2048]{1,0:T(8,128)(2,1)} %weight.3), custom_call_target="tpu_custom_call" | custom-call | tf_op jit(solution)/shard_map/fetch/pallas_call | solution.py:265
  74.5 90.9 %attend.1 = (bf16[8,32,64,128]{3,2,1,0:T(8,128)(2,1)}, bf16[256,2048]{1,0:T(8,128)(2,1)}, f32[16,2048]{1,0:T(8,128)}, bf16[256,2048]{1,0:T(8,128)(2,1)}, bf16[16...) custom-call(s32[8,256]{1,0:T(8,128)} %shard_map.110.tab, s32[1,16]{1,0:T(1,128)} %bitcast.1, ...), custom_call_target="tpu_custom_call" | custom-call | tf_op jit(solution)/shard_map/attend/pallas_call | solution.py:585
  165.4 6.3 %finish.1 = (bf16[256,2048]{1,0:T(8,128)(2,1)}, bf16[256,2048]{1,0:T(8,128)(2,1)}, bf16[256,2048]{1,0:T(8,128)(2,1)}, bf16[256,2048]{1,0:T(8,128)(2,1)}, f32[16,2048]{1,0:T(8,128)}) custom-call(s32[8,256]{1,0:T(8,128)} %shard_map.110.tab, bf16[8,32,64,128]{3,2,1,0:T(8,128)(2,1)} %get-tuple-element.22.back_k.back_v, ...), custom_call_target="tpu_custom_call" | custom-call | tf_op jit(solution)/shard_map/finish/pallas_call | solution.py:661

commit v4 on v3

--- a/solution.py
+++ b/solution.py
@@ -22,7 +22,7 @@
 PAIR = 4
 EARLY = 4
 TILES = 8
-LATE = 7
+LATE = 0
 WHEN = ((7, 9), (6, 7), (6, 7))
 SCALE = 1.0 / math.sqrt(DH)
 MESH = pl.DeviceIdType.MESH
@@ -539,9 +539,6 @@
     ]
     for p in range(PARTS):
         return_y(p)
-        if p == LATE:
-            partial(0)
-    send_one(0)
     each = HEADS // PARTS
     for p in range(PARTS):
         return_x(p)
@@ -551,6 +548,9 @@
             loads[7].wait()
             lax.fori_loop(0, 8, layer_tile, 0)
             stores[3].start()
+        if p == LATE:
+            partial(0)
+            send_one(0)
         lax.fori_loop(p * each, (p + 1) * each, backward_own, 0, unroll=each)
         for level, step in enumerate((sum_one, sum_two)):
             for n in range(3):

time: 173 us -> 172 us (level)
  no operation moved by 1% of the time
where the time goes in v4:
time: 172 us
  Pallas kernels  171 us (99%)
    pallas_call x1, Pallas kernels, attend(): pl.pallas_call(attend_kernel, out_shape=(jax.ShapeDtypeStruct((PARTS, 32,...  91.1 us
    pallas_call x1, Pallas kernels, fetch(): pl.pallas_call(fetch_kernel, out_shape=(jax.ShapeDtypeStruct((PARTS, 16,...  72 us
    pallas_call x1, Pallas kernels, finish(): pl.pallas_call(final_kernel, out_shape=(tokens, tokens, tokens, tokens, j...  6.26 us

profile of v4, /device:TPU:1, one launch (start us, length us, event | category | flops | bytes accessed | tf_op | source)
XLA Modules:
  0.0 172.0 jit_solution(10161098188929960478)
XLA Ops:
  0.6 1.9 %shard_map.110.tab = s32[8,256]{1,0:T(8,128)} custom-call(s32[16,128]{1,0:T(8,128)} %src_ref.1), custom_call_target="tpu_custom_call" | custom-call | tf_op jit(solution)/shard_map/pallas_call | solution.py:143
  2.5 72.0 %fetch.1 = (bf16[8,16,64,128]{3,2,1,0:T(8,128)(2,1)}, bf16[256,2048]{1,0:T(8,128)(2,1)}, bf16[256,2048]{1,0:T(8,128)(2,1)}) custom-call(s32[8,256]{1,0:T(8,128)} %shard_map.110.tab, bf16[256,2048]{1,0:T(8,128)(2,1)} %key.3, bf16[256,2048]{1,0:T(8,128)(2,1)} %value.3, bf16[256,2048]{1,0:T(8,128)(2,1)} %cot_in.1, bf16[2048,2048]{1,0:T(8,128)(2,1)} %weight.3), custom_call_target="tpu_custom_call" | custom-call | tf_op jit(solution)/shard_map/fetch/pallas_call | solution.py:265
  74.5 91.1 %attend.1 = (bf16[8,32,64,128]{3,2,1,0:T(8,128)(2,1)}, bf16[256,2048]{1,0:T(8,128)(2,1)}, f32[16,2048]{1,0:T(8,128)}, bf16[256,2048]{1,0:T(8,128)(2,1)}, bf16[16...) custom-call(s32[8,256]{1,0:T(8,128)} %shard_map.110.tab, s32[1,16]{1,0:T(1,128)} %bitcast.1, ...), custom_call_target="tpu_custom_call" | custom-call | tf_op jit(solution)/shard_map/attend/pallas_call | solution.py:585
  165.6 6.3 %finish.1 = (bf16[256,2048]{1,0:T(8,128)(2,1)}, bf16[256,2048]{1,0:T(8,128)(2,1)}, bf16[256,2048]{1,0:T(8,128)(2,1)}, bf16[256,2048]{1,0:T(8,128)(2,1)}, f32[16,2048]{1,0:T(8,128)}) custom-call(s32[8,256]{1,0:T(8,128)} %shard_map.110.tab, bf16[8,32,64,128]{3,2,1,0:T(8,128)(2,1)} %get-tuple-element.22.back_k.back_v, ...), custom_call_target="tpu_custom_call" | custom-call | tf_op jit(solution)/shard_map/finish/pallas_call | solution.py:661
